TPU v7x, 32 devices: a whole 2x2x4 slice. The times are simulated.
32 devices in a mesh: col: 8 (over y, x, core), row: 4 (over z).
Axes of the slice: x: 2, y: 2, z: 4, core: 2. Of those that a mesh axis runs over, the one named last changes fastest.
Arguments:
- kernel: float32 [512, 1024, 256], P('row', 'col'), may hold values from -0.01171875 to 0.01171875
- history: float32 [1024, 16, 256], P(('col', 'row')), may hold values from -6 to 6
- noise_weight: float32 [512, 256], P('row'), may hold values from 0.3 to 3
- prior_weight: float32 [1024], P(('col', 'row')), may hold values from 0.3 to 3
Outputs:
- hessian_action: float32 [1024, 16, 256], P(('col', 'row'))
All inputs are finite; a program needn't handle non-finite values.
Results may differ from a plain program's by a relative error of at most 0.00005.
Values sent between devices are 32-bit elements; how exact they have to be, the bound alone decides.
A program may use at most 192 MiB of HBM per device.

v0:
```python
import math

import jax
import jax.numpy as jnp
from jax import lax
from jax.sharding import PartitionSpec as P

exact_mode = lax.Precision.HIGHEST


def dft_tables(steps_total):
    length = 2 * steps_total
    times_col = jnp.arange(steps_total, dtype=jnp.int32)[:, None]
    freq_row = jnp.arange(length, dtype=jnp.int32)[None, :]
    phase = (times_col * freq_row % length).astype(jnp.float32) * (2.0 * math.pi / length)
    return (jnp.cos(phase), jnp.sin(phase))


def local(kernel, history, noise_weight, prior_weight):
    steps_total = history.shape[2]
    length = 2 * steps_total
    cos_table, sin_table = dft_tables(steps_total)
    kernel_real = jnp.einsum("spk,kf->spf", kernel, cos_table, precision=exact_mode)
    kernel_imag = -jnp.einsum("spk,kf->spf", kernel, sin_table, precision=exact_mode)

    def to_time(spec_real, spec_imag):
        return (
            jnp.einsum("abf,tf->abt", spec_real, cos_table, precision=exact_mode)
            - jnp.einsum("abf,tf->abt", spec_imag, sin_table, precision=exact_mode)
        ) / length

    shard_rows = lax.all_gather(history, "row", axis=0, tiled=True)
    part_real = kernel_real
    part_imag = kernel_imag
    hist_real = jnp.einsum("prk,kf->prf", shard_rows, cos_table, precision=exact_mode)
    hist_imag = -jnp.einsum("prk,kf->prf", shard_rows, sin_table, precision=exact_mode)
    new_real = jnp.einsum("spf,prf->srf", part_real, hist_real, precision=exact_mode) - jnp.einsum(
        "spf,prf->srf", part_imag, hist_imag, precision=exact_mode
    )
    new_imag = jnp.einsum("spf,prf->srf", part_real, hist_imag, precision=exact_mode) + jnp.einsum(
        "spf,prf->srf", part_imag, hist_real, precision=exact_mode
    )
    spec_real = new_real
    spec_imag = new_imag
    partial_data = to_time(spec_real, spec_imag)
    data = lax.psum(partial_data, "col")
    weighted = data * noise_weight[:, None, :]
    weighted_real = jnp.einsum("srk,kf->srf", weighted, cos_table, precision=exact_mode)
    weighted_imag = -jnp.einsum("srk,kf->srf", weighted, sin_table, precision=exact_mode)
    part_real = kernel_real
    part_imag = kernel_imag
    grad_real = jnp.einsum(
        "spf,srf->prf", part_real, weighted_real, precision=exact_mode
    ) + jnp.einsum("spf,srf->prf", part_imag, weighted_imag, precision=exact_mode)
    grad_imag = jnp.einsum(
        "spf,srf->prf", part_real, weighted_imag, precision=exact_mode
    ) - jnp.einsum("spf,srf->prf", part_imag, weighted_real, precision=exact_mode)
    gradient = lax.psum_scatter(
        to_time(grad_real, grad_imag), "row", scatter_dimension=0, tiled=True
    )
    return gradient + prior_weight[:, None, None] * history


def solution(mesh):
    in_specs = (
        P("row", "col", None),
        P(("col", "row"), None, None),
        P("row", None),
        P(("col", "row")),
    )
    out_specs = P(("col", "row"), None, None)
    return jax.shard_map(local, mesh=mesh, in_specs=in_specs, out_specs=out_specs, check_vma=False)
```

profile of v0, /device:TPU:0, one launch (start us, length us, event | category | flops | bytes accessed | tf_op | source)
XLA Modules:
  0.0 908.3 jit_solution(8476181982117455981)
XLA Ops:
  6.5 0.0 all-gather.2.cloned.1.call-start
  6.5 2.1 copy.5
  8.7 0.0 all-gather.2.cloned.1.call-update
  8.7 0.0 all-reduce.2.cloned.1.call-start
  8.8 1.9 fusion.123
  10.7 59.3 %negate_bitcast_fusion = f32[128,128,512]{1,2,0:T(8,128)} fusion(f32[128,128,256]{2,1,0:T(8,128)} %param.4, f32[256,512,1]{1,0,2:T(8,128)S(1)} %fusion.123), kind=kOutput, calls=%fused_computation | convolution fusion | flops 25778192384 | bytes 50855936 | tf_op jit(solution)/shard_map/spk,kf->spf/dot_general | solution.py:24
  70.0 1.9 fusion.125
  71.9 59.1 %convolution_bitcast_fusion = f32[128,128,512]{1,2,0:T(8,128)} fusion(f32[128,128,256]{2,1,0:T(8,128)} %param.4, f32[256,512,1]{1,0,2:T(8,128)S(1)} %fusion.125), kind=kOutput, calls=%fused_computation.17 | convolution fusion | flops 25769803776 | bytes 50855936 | tf_op jit(solution)/shard_map/spk,kf->spf/dot_general | solution.py:23
  131.0 0.0 all-gather.2.cloned.1.call-done
  131.0 10.1 %negate_bitcast_fusion.1 = f32[128,16,512]{0,2,1:T(8,128)S(1)} fusion(f32[128,16,256]{2,0,1:T(8,128)} %all-gather.2.cloned.1.call-done), kind=kOutput, calls=%fused_computation.30 | convolution fusion | flops 3224109056 | bytes 6291456 | tf_op jit(solution)/shard_map/prk,kf->prf/dot_general | solution.py:36
  141.2 0.0 copy-start.6
  141.2 79.6 %fusion.2 = f32[512,16,128]{2,1,0:T(8,128)} fusion(f32[128,128,512]{1,2,0:T(8,128)} %negate_bitcast_fusion, f32[128,16,512]{0,2,1:T(8,128)S(1)} %negate_bitcast_fusion.1), kind=kOutput, calls=%fused_computation.3 | convolution fusion | flops 1610612736 | bytes 41943040 | tf_op jit(solution)/shard_map/spf,prf->srf/dot_general | solution.py:37
  220.8 0.0 copy-done.6
  220.8 8.5 convolution_bitcast_fusion.1
  229.3 80.9 %fusion = f32[512,16,128]{2,1,0:T(8,128)} fusion(f32[128,128,512]{1,2,0:T(8,128)} %negate_bitcast_fusion, f32[128,16,512]{0,2,1:T(8,128)S(1)} %convolution_bitcast_fusion.1), kind=kOutput, calls=%fused_computation.1 | convolution fusion | flops 1610612736 | bytes 41943040 | tf_op jit(solution)/shard_map/spf,prf->srf/dot_general | solution.py:40
  310.2 79.0 %fusion.10 = f32[512,16,128]{2,1,0:T(8,128)} fusion(f32[128,128,512]{1,2,0:T(8,128)} %convolution_bitcast_fusion, f32[128,16,512]{0,2,1:T(8,128)S(1)} %convolution_bitcast_fusion.1), kind=kOutput, calls=%fused_computation.11 | convolution fusion | flops 1610612736 | bytes 41943040 | tf_op jit(solution)/shard_map/spf,prf->srf/dot_general | solution.py:37
  389.2 79.2 %fusion.8 = f32[512,16,128]{2,1,0:T(8,128)} fusion(f32[128,128,512]{1,2,0:T(8,128)} %convolution_bitcast_fusion, f32[128,16,512]{0,2,1:T(8,128)S(1)} %negate_bitcast_fusion.1), kind=kOutput, calls=%fused_computation.9 | convolution fusion | flops 1610612736 | bytes 41943040 | tf_op jit(solution)/shard_map/spf,prf->srf/dot_general | solution.py:40
  468.3 5.3 copy.21
  473.6 5.3 copy.23
  478.9 5.3 copy.16
  484.2 5.3 copy.22
  489.5 9.0 fusion.20
  498.5 0.0 copy-start.9
  498.5 6.8 subtract_multiply_fusion.1
  505.4 0.0 all-reduce.2.cloned.1.call-update
  505.4 0.0 reduce-scatter.2.cloned.1.call-start
  505.4 64.2 %all-reduce.2.cloned.1.call-done = f32[128,16,256]{2,0,1:T(8,128)} async-done(((f32[128,16,256]{2,0,1:T(8,128)}), f32[128,16,256]{2,0,1:T(8,128)}) %all-reduce.2.cloned.1.call-update) | async-done | bytes 2097168 | tf_op jit(solution)/shard_map/psum | solution.py:46
  569.7 8.6 convolution_negate_fusion
  578.3 5.5 copy.27
  583.8 55.4 %fusion.6 = f32[512,16,128]{2,1,0:T(8,128)} fusion(f32[128,16,512]{0,1,2:T(8,128)} %copy.27, f32[128,128,512]{1,2,0:T(8,128)} %negate_bitcast_fusion), kind=kOutput, calls=%fused_computation.7 | convolution fusion | flops 1610612736 | bytes 41943040 | tf_op jit(solution)/shard_map/spf,srf->prf/dot_general | solution.py:54
  639.1 56.1 %fusion.12 = f32[512,16,128]{2,1,0:T(8,128)} fusion(f32[128,16,512]{0,1,2:T(8,128)S(1)} %copy-done.1, f32[128,128,512]{1,2,0:T(8,128)} %convolution_bitcast_fusion), kind=kOutput, calls=%fused_computation.13 | convolution fusion | flops 1610612736 | bytes 41943040 | tf_op jit(solution)/shard_map/spf,srf->prf/dot_general | solution.py:55
  695.2 0.0 copy-done.7
  695.2 7.0 fusion.33
  702.2 5.4 copy.24
  707.6 55.2 %fusion.4 = f32[512,16,128]{2,1,0:T(8,128)} fusion(f32[128,16,512]{0,1,2:T(8,128)} %copy.24, f32[128,128,512]{1,2,0:T(8,128)} %negate_bitcast_fusion), kind=kOutput, calls=%fused_computation.5 | convolution fusion | flops 1610612736 | bytes 41943040 | tf_op jit(solution)/shard_map/spf,srf->prf/dot_general | solution.py:57
  762.9 55.8 %fusion.14 = f32[512,16,128]{2,1,0:T(8,128)} fusion(f32[128,16,512]{0,1,2:T(8,128)S(1)} %copy-done, f32[128,128,512]{1,2,0:T(8,128)} %convolution_bitcast_fusion), kind=kOutput, calls=%fused_computation.15 | convolution fusion | flops 1610612736 | bytes 41943040 | tf_op jit(solution)/shard_map/spf,srf->prf/dot_general | solution.py:52
  818.7 5.3 copy.26
  824.0 5.3 copy.30
  829.3 5.3 copy.29
  834.6 5.2 copy.31
  839.9 9.0 fusion.16
  849.0 0.0 copy-start.8
  849.0 0.0 copy-start.10
  849.0 6.8 subtract_multiply_fusion
  855.8 0.0 reduce-scatter.2.cloned.1.call-update
  855.8 43.2 %reduce-scatter.2.cloned.1.call-done = f32[32,16,256]{2,0,1:T(8,128)} async-done(((f32[128,16,256]{2,0,1:T(8,128)}), f32[32,16,256]{2,0,1:T(8,128)}) %reduce-scatter.2.cloned.1.call-update) | async-done | bytes 524304 | tf_op jit(solution)/shard_map/reduce_scatter | solution.py:58
  899.1 1.4 multiply_add_fusion
  900.4 1.1 copy.11
  (16 shorter events, 0.0 us)
Async XLA Ops:
  6.5 124.5 %all-gather.2.cloned.1.call-start = ((), (), s32[]{:S(2)}) async-start(), calls=%async_computation.1 | async-start | bytes 2621440 | tf_op jit(solution)/shard_map/all_gather | solution.py:32
  8.7 561.0 %all-reduce.2.cloned.1.call-start = ((), (), s32[]{:S(2)}) async-start(), calls=%async_computation.2 | async-start | bytes 4194304 | tf_op jit(solution)/shard_map/psum | solution.py:46
  141.2 79.6 %copy-start.6 = (f32[128,16,256]{2,0,1:T(8,128)S(1)}, f32[128,16,256]{2,0,1:T(8,128)}, u32[]{:S(2)}) copy-start(f32[128,16,256]{2,0,1:T(8,128)} %all-gather.2.cloned.1.call-done) | copy-start | bytes 6291460
  489.5 9.0 copy-start.2
  489.5 9.0 copy-start.4
  498.5 71.2 %copy-start.9 = (f32[128,256]{1,0:T(8,128)S(1)}, f32[128,256]{1,0:T(8,128)}, u32[]{:S(2)}) copy-start(f32[128,256]{1,0:T(8,128)} %param.6) | copy-start | bytes 393220
  505.4 393.7 %reduce-scatter.2.cloned.1.call-start = ((), (), s32[]{:S(2)}) async-start(), calls=%async_computation.3 | async-start | bytes 2621440 | tf_op jit(solution)/shard_map/reduce_scatter | solution.py:58
  583.8 55.4 %copy-start.1 = (f32[128,16,512]{0,1,2:T(8,128)S(1)}, f32[128,16,512]{0,1,2:T(8,128)}, u32[]{:S(2)}) copy-start(f32[128,16,512]{0,1,2:T(8,128)} %copy.27) | copy-start | bytes 12582916
  639.1 56.1 %copy-start.7 = (f32[128,16,256]{2,0,1:T(8,128)S(1)}, f32[128,16,256]{2,0,1:T(8,128)}, u32[]{:S(2)}) copy-start(f32[128,16,256]{2,0,1:T(8,128)} %all-reduce.2.cloned.1.call-done) | copy-start | bytes 6291460
  707.6 55.2 %copy-start = (f32[128,16,512]{0,1,2:T(8,128)S(1)}, f32[128,16,512]{0,1,2:T(8,128)}, u32[]{:S(2)}) copy-start(f32[128,16,512]{0,1,2:T(8,128)} %copy.24) | copy-start | bytes 12582916
  839.9 9.0 copy-start.3
  839.9 9.1 copy-start.5
  849.0 50.1 %copy-start.8 = (f32[32,16,256]{2,1,0:T(8,128)S(1)}, f32[32,16,256]{2,1,0:T(8,128)}, u32[]{:S(2)}) copy-start(f32[32,16,256]{2,1,0:T(8,128)} %param.5) | copy-start | bytes 1572868
  849.0 50.1 %copy-start.10 = (f32[32]{0:T(128)S(1)}, f32[32]{0:T(128)}, u32[]{:S(2)}) copy-start(f32[32]{0:T(128)} %param.7) | copy-start | bytes 388
Sparse Core Ops, SparseCore 0:
  8.9 48.6 all-gather.1
  505.5 64.1 all-reduce.1
  856.0 43.0 reduce-scatter.1
where the time goes:
time: 912 us; the launch traced here: 908 us
  matrix products  725 us (79%)
  waiting for transfers between devices  108 us (12%)
  local copies, waits for them, and re-layouts  56.5 us (6%)
  between operations  13.5 us (1%)
    dot_general x1, matrix products, local(): jnp.einsum('spf,prf->srf', part_imag, hist_real, precision=exact_mode)  80.9 us
    dot_general x1, matrix products, local(): jnp.einsum('spf,prf->srf', part_imag, hist_imag, precision=exact_mode)  79.6 us
    dot_general x1, matrix products, local(): jnp.einsum('spf,prf->srf', part_real, hist_imag, precision=exact_mode)  79.2 us
    dot_general x1, matrix products, local(): jnp.einsum('spf,prf->srf', part_real, hist_real, precision=exact_mode)  79 us
    psum x1, waiting for transfers between devices, local(): data = lax.psum(partial_data, 'col')  64.2 us
    dot_general x1, matrix products, local(): jnp.einsum('spk,kf->spf', kernel, sin_table, precision=exact_mode)  59.3 us
    dot_general x1, matrix products, local(): jnp.einsum('spk,kf->spf', kernel, cos_table, precision=exact_mode)  59.1 us
    dot_general x1, matrix products, local(): jnp.einsum('spf,srf->prf', part_real, weighted_imag, precision=exact_mode)  56.1 us
  transfers between devices with their start and end apart: 3, of which 2 were waited for; matrix products, arithmetic and copies ran while one was open for 13% of the time, Pallas kernels for 0%

commit v1 on v0

v1 whole, which is shorter than its diff:
```python
import functools
import math

import jax
import jax.numpy as jnp
import ml_dtypes
import numpy as np
from jax import lax
from jax.experimental import pallas as pl
from jax.experimental.pallas import tpu as pltpu
from jax.sharding import PartitionSpec as P

f32 = jnp.float32
bf16 = jnp.bfloat16
VMEM_LIMIT = 48 * 1024 * 1024
SENSOR_BLOCK = 16
FREQ_BLOCK = 16


def transform_table(steps):
    freqs = np.arange(steps, dtype=np.int64)[:, None]
    times = np.arange(steps, dtype=np.int64)[None, :]
    phase = ((2 * freqs + 1) * times % (4 * steps)).astype(np.float64) * (math.pi / (2 * steps))
    return np.concatenate([np.cos(phase), -np.sin(phase)], axis=0)


def split_host(table):
    table = table.astype(np.float32)
    high = table.astype(ml_dtypes.bfloat16)
    low = (table - high.astype(np.float32)).astype(ml_dtypes.bfloat16)
    return high, low


def split(value):
    high = value.astype(bf16)
    return high, (value - high.astype(f32)).astype(bf16)


def matmul(lhs, rhs):
    return lax.dot_general(lhs, rhs, (((1,), (0,)), ((), ())), preferred_element_type=f32)


def matmul_nt(lhs, rhs):
    return lax.dot_general(lhs, rhs, (((1,), (1,)), ((), ())), preferred_element_type=f32)


def kernel_transform(table_ref, kernel_ref, out_ref, real_ref, imag_ref):
    sensors, params, steps = kernel_ref.shape
    for s in range(0, sensors, 2):
        high, low = split(kernel_ref[s : s + 2].reshape(2 * params, steps))
        spec = matmul_nt(table_ref[...], jnp.concatenate([high, low, high], axis=1))
        for j in range(2):
            cols = slice(j * params, (j + 1) * params)
            real_ref[pl.ds(s + j, steps, stride=sensors), :] = spec[:steps, cols]
            imag_ref[pl.ds(s + j, steps, stride=sensors), :] = spec[steps:, cols]

    group = 8

    def emit(i, carry):
        rows = pl.ds(pl.multiple_of(i * group * sensors, group * sensors), group * sensors)
        freqs = pl.ds(i * group, group)
        for part, ref in enumerate((real_ref, imag_ref)):
            high, low = split(ref[rows, :].reshape(group, sensors, params))
            out_ref[freqs, 0, :, part * params : (part + 1) * params] = high
            out_ref[freqs, 1, :, part * params : (part + 1) * params] = low
        return carry

    lax.fori_loop(0, steps // group, emit, 0)


def forward(table_ref, inverse_ref, hist_ref, khat_ref, out_ref, hreal_ref, himag_ref, data_ref):
    step = pl.program_id(0)
    blocks, vectors, part_params, steps = hist_ref.shape
    params = blocks * part_params
    freq_block, _, sensors, _ = khat_ref.shape

    @pl.when(step == 0)
    def _():
        for r in range(0, vectors, 2):
            hist = jnp.concatenate([hist_ref[:, r + j].reshape(params, steps) for j in range(2)], axis=0)
            high, low = split(hist)
            spec = matmul_nt(table_ref[...], jnp.concatenate([high, low, high], axis=1))
            for j in range(2):
                cols = slice(j * params, (j + 1) * params)
                hreal_ref[pl.ds(r + j, steps, stride=vectors), :] = spec[:steps, cols]
                himag_ref[pl.ds(r + j, steps, stride=vectors), :] = spec[steps:, cols]

    for i in range(freq_block):
        f = step * freq_block + i
        rows = pl.ds(pl.multiple_of(f * vectors, vectors), vectors)
        real, imag = hreal_ref[rows, :], himag_ref[rows, :]
        both = jnp.concatenate(
            [jnp.concatenate([real, -imag], axis=1), jnp.concatenate([imag, real], axis=1)], axis=0
        )
        lhs = jnp.concatenate(split(both), axis=0)
        res = matmul_nt(lhs, khat_ref[i].reshape(2 * sensors, 2 * params))
        top, bottom = res[: 2 * vectors], res[2 * vectors :]
        data_ref[pl.ds(pl.multiple_of(f * 2 * vectors, 2 * vectors), 2 * vectors), :] = (
            top[:, :sensors] + (top[:, sensors:] + bottom[:, :sensors])
        )

    @pl.when(step == pl.num_programs(0) - 1)
    def _():
        for r in range(0, vectors, 2):
            spec = jnp.concatenate(
                [
                    jnp.concatenate(
                        [data_ref[pl.ds(part * vectors + r + j, steps, stride=2 * vectors), :] for j in range(2)],
                        axis=1,
                    )
                    for part in range(2)
                ],
                axis=0,
            )
            high, low = split(spec)
            times = matmul(inverse_ref[...], jnp.concatenate([high, low, high], axis=0))
            for j in range(2):
                out_ref[r + j] = times[:, j * sensors : (j + 1) * sensors]


def adjoint(table_ref, inverse_ref, data_ref, noise_ref, khat_ref, out_ref, spec_ref, grad_ref):
    step = pl.program_id(0)
    vectors, steps, sensors = data_ref.shape
    freq_block, params = khat_ref.shape[0], khat_ref.shape[3] // 2
    blocks, _, part_params, _ = out_ref.shape

    @pl.when(step == 0)
    def _():
        for r in range(0, vectors, 2):
            weighted = jnp.concatenate([data_ref[r + j] * noise_ref[...] for j in range(2)], axis=1)
            high, low = split(weighted)
            spec = matmul(table_ref[...], jnp.concatenate([high, low, high], axis=0))
            for j in range(2):
                cols = slice(j * sensors, (j + 1) * sensors)
                spec_ref[pl.ds(r + j, steps, stride=2 * vectors), :] = spec[:steps, cols]
                spec_ref[pl.ds(vectors + r + j, steps, stride=2 * vectors), :] = spec[steps:, cols]

    for i in range(freq_block):
        f = step * freq_block + i
        base = pl.multiple_of(f * 2 * vectors, 2 * vectors)
        high, low = split(spec_ref[pl.ds(base, 2 * vectors), :])
        lhs = jnp.concatenate(
            [jnp.concatenate([high, high], axis=1), jnp.concatenate([low, jnp.zeros_like(low)], axis=1)], axis=0
        )
        res = matmul(lhs, khat_ref[i].reshape(2 * sensors, 2 * params))
        res = res[: 2 * vectors] + res[2 * vectors :]
        grad_ref[pl.ds(base, vectors), :] = res[:vectors, :params] + res[vectors:, params:]
        grad_ref[pl.ds(base + vectors, vectors), :] = res[vectors:, :params] - res[:vectors, params:]

    @pl.when(step == pl.num_programs(0) - 1)
    def _():
        for r in range(0, vectors, 2):
            spec = jnp.concatenate(
                [
                    jnp.concatenate(
                        [grad_ref[pl.ds(part * vectors + r + j, steps, stride=2 * vectors), :] for part in range(2)],
                        axis=0,
                    ).T
                    for j in range(2)
                ],
                axis=0,
            )
            high, low = split(spec)
            times = matmul(jnp.concatenate([high, low, high], axis=1), inverse_ref[...])
            for j in range(2):
                out_ref[:, r + j] = times[j * params : (j + 1) * params].reshape(blocks, part_params, steps)


def local(row_count, kernel, history, noise_weight, prior_weight):
    sensors, params, steps = kernel.shape
    part_params, vectors, _ = history.shape
    pad = -sensors % 128
    if pad:
        kernel = jnp.pad(kernel, ((0, pad), (0, 0), (0, 0)))
        noise_weight = jnp.pad(noise_weight, ((0, pad), (0, 0)))
        sensors += pad

    table = transform_table(steps)
    th, tl = split_host(table)
    ih, il = split_host(table / steps)
    table_k = jnp.asarray(np.concatenate([th, th, tl], axis=1))
    inverse_t = jnp.asarray(np.concatenate([ih.T, ih.T, il.T], axis=1))
    inverse_f = jnp.asarray(np.concatenate([ih, ih, il], axis=0))

    whole = lambda *shape: pl.BlockSpec(shape, lambda i: (0,) * len(shape))
    params_of = pltpu.CompilerParams(vmem_limit_bytes=VMEM_LIMIT)

    moved = history.transpose(1, 0, 2)
    gathered = lax.all_gather(moved, "row", axis=0)

    khat = pl.pallas_call(
        kernel_transform,
        grid=(sensors // SENSOR_BLOCK,),
        in_specs=[
            whole(2 * steps, 3 * steps),
            pl.BlockSpec((SENSOR_BLOCK, params, steps), lambda i: (i, 0, 0)),
        ],
        out_specs=pl.BlockSpec((steps, 2, SENSOR_BLOCK, 2 * params), lambda i: (0, 0, i, 0)),
        out_shape=jax.ShapeDtypeStruct((steps, 2, sensors, 2 * params), bf16),
        scratch_shapes=[pltpu.VMEM((steps * SENSOR_BLOCK, params), f32)] * 2,
        compiler_params=params_of,
        cost_estimate=pl.CostEstimate(
            flops=12 * sensors * params * steps * steps,
            bytes_accessed=12 * sensors * params * steps,
            transcendentals=0,
        ),
        name="kernel_transform",
    )(table_k, kernel)

    khat_spec = pl.BlockSpec((FREQ_BLOCK, 2, sensors, 2 * params), lambda i: (i, 0, 0, 0))
    freq_cost = pl.CostEstimate(
        flops=16 * vectors * sensors * params * steps,
        bytes_accessed=8 * sensors * params * steps,
        transcendentals=0,
    )
    partial = pl.pallas_call(
        forward,
        grid=(steps // FREQ_BLOCK,),
        in_specs=[
            whole(2 * steps, 3 * steps),
            whole(steps, 6 * steps),
            whole(row_count, vectors, part_params, steps),
            khat_spec,
        ],
        out_specs=whole(vectors, steps, sensors),
        out_shape=jax.ShapeDtypeStruct((vectors, steps, sensors), f32),
        scratch_shapes=[
            pltpu.VMEM((steps * vectors, params), f32),
            pltpu.VMEM((steps * vectors, params), f32),
            pltpu.VMEM((steps * 2 * vectors, sensors), f32),
        ],
        compiler_params=params_of,
        cost_estimate=freq_cost,
        name="forward",
    )(table_k, inverse_t, gathered, khat)

    data = lax.psum(partial, "col")

    grad = pl.pallas_call(
        adjoint,
        grid=(steps // FREQ_BLOCK,),
        in_specs=[
            whole(2 * steps, 3 * steps),
            whole(6 * steps, steps),
            whole(vectors, steps, sensors),
            whole(steps, sensors),
            khat_spec,
        ],
        out_specs=whole(row_count, vectors, part_params, steps),
        out_shape=jax.ShapeDtypeStruct((row_count, vectors, part_params, steps), f32),
        scratch_shapes=[
            pltpu.VMEM((steps * 2 * vectors, sensors), f32),
            pltpu.VMEM((steps * 2 * vectors, params), f32),
        ],
        compiler_params=params_of,
        cost_estimate=freq_cost,
        name="adjoint",
    )(table_k, inverse_f, data, noise_weight.T, khat)

    gradient = lax.psum_scatter(grad, "row", scatter_dimension=0, tiled=False)
    return gradient.transpose(1, 0, 2) + prior_weight[:, None, None] * history


def solution(mesh):
    in_specs = (
        P("row", "col", None),
        P(("col", "row"), None, None),
        P("row", None),
        P(("col", "row")),
    )
    out_specs = P(("col", "row"), None, None)
    return jax.shard_map(
        functools.partial(local, mesh.shape["row"]),
        mesh=mesh,
        in_specs=in_specs,
        out_specs=out_specs,
        check_vma=False,
    )
```

time: 912 us -> 231 us (0.25)
  matrix products: 725 us -> 0 us
  Pallas kernels: 0 us -> 86 us
  local copies, waits for them, and re-layouts: 56.5 us -> 7.38 us
  waiting for transfers between devices: 108 us -> 122 us
    dot_general x18 -> x0, matrix products: 725 us -> none  [the longest x1 80.9 us: local(): jnp.einsum('spf,prf->srf', part_imag, hist_real, precision=exact_mode)]
    pallas_call x0 -> x3, Pallas kernels: none -> 86 us  [the longest x1 30.7 us: local(): pl.pallas_call(kernel_transform, grid=(sensors // SENSOR_BLOCK,), in_spec...]
    dot_general x9 -> x0, local copies, waits for them, and re-layouts: 47.7 us -> none  [the longest x1 5.44 us: local(): jnp.einsum('srk,kf->srf', weighted, cos_table, precision=exact_mode)]
    all_gather x1, waiting for transfers between devices: 0.02 us -> 18.4 us  [local(): gathered = lax.all_gather(moved, 'row', axis=0)]
  transfers between devices with their start and end apart: 3 -> 3, of which waited for: 2 -> 3; matrix products, arithmetic and copies ran while one was open for 13% -> 0% of each run, Pallas kernels for 0% -> 13%
where the time goes in v1:
time: 231 us; the launch traced here: 230 us
  waiting for transfers between devices  122 us (53%)
  Pallas kernels  86 us (37%)
  between operations  13.2 us (6%)
  local copies, waits for them, and re-layouts  7.38 us (3%)
    psum x1, waiting for transfers between devices, local(): data = lax.psum(partial, 'col')  59.3 us
    reduce_scatter x1, waiting for transfers between devices, local(): gradient = lax.psum_scatter(grad, 'row', scatter_dimension=0, tiled=False)  43.2 us
    pallas_call x1, Pallas kernels, local(): pl.pallas_call(kernel_transform, grid=(sensors // SENSOR_BLOCK,), in_spec...  30.7 us
    pallas_call x1, Pallas kernels, local(): pl.pallas_call(forward, grid=(steps // FREQ_BLOCK,), in_specs=[whole(2 *...  28.3 us
    pallas_call x1, Pallas kernels, local(): pl.pallas_call(adjoint, grid=(steps // FREQ_BLOCK,), in_specs=[whole(2 *...  27 us
    all_gather x1, waiting for transfers between devices, local(): gathered = lax.all_gather(moved, 'row', axis=0)  18.4 us
  transfers between devices with their start and end apart: 3, of which 3 were waited for; matrix products, arithmetic and copies ran while one was open for 0% of the time, Pallas kernels for 13%

profile of v1, /device:TPU:0, one launch (start us, length us, event | category | flops | bytes accessed | tf_op | source)
XLA Modules:
  0.0 230.0 jit_solution(12295011933847902160)
XLA Ops:
  6.5 0.0 all-gather.3.cloned.1.call-start
  6.5 0.7 all-gather.3.cloned.1.call-update
  7.3 0.0 all-reduce.2.cloned.1.call-start
  7.3 0.0 copy-start
  7.3 1.1 copy-done
  8.4 30.7 %kernel_transform.1.khat_ref = bf16[256,2,128,256]{3,2,1,0:T(8,128)(2,1)} custom-call(bf16[512,768]{1,0:T(8,128)(2,1)S(1)} %copy-done, f32[128,128,256]{2,1,0:T(8,128)} %kernel_ref.1), custom_call_target="tpu_custom_call" | custom-call | flops 12884901888 | bytes 50331648 | tf_op jit(solution)/shard_map/kernel_transform/pallas_call | solution.py:191
  39.1 0.0 copy-start.1
  39.2 0.0 copy-start.4
  39.2 18.4 %all-gather.3.cloned.1.call-done = f32[64,32,256]{2,0,1:T(8,128)} async-done(((f32[16,32,256]{2,0,1:T(8,128)}), f32[64,32,256]{2,0,1:T(8,128)}) %all-gather.3.cloned.1.call-update) | async-done | bytes 2097168 | tf_op jit(solution)/shard_map/all_gather | solution.py:189
  57.6 2.8 %copy.8 = f32[64,32,256]{2,1,0:T(8,128)S(1)} copy(f32[64,32,256]{2,0,1:T(8,128)} %all-gather.3.cloned.1.call-done) | data formatting | bytes 4194304 | tf_op jit(solution)/shard_map/all_gather | solution.py:189
  60.4 0.0 copy-done.1
  60.4 0.0 copy-done.4
  60.4 28.3 %forward.1 = f32[16,256,128]{2,1,0:T(8,128)} custom-call(bf16[512,768]{1,0:T(8,128)(2,1)S(1)} %copy-done.1, bf16[256,1536]{1,0:T(8,128)(2,1)S(1)} %copy-done.4, f32[4,16,32,256]{3,2,1,0:T(8,128)S(1)} %bitcast.7, bf16[256,2,128,256]{3,2,1,0:T(8,128)(2,1)} %kernel_transform.1.khat_ref), custom_call_target="tpu_custom_call" | custom-call | flops 1073741824 | bytes 33554432 | tf_op jit(solution)/shard_map/forward/pallas_call | solution.py:216
  88.7 0.0 copy-start.6
  88.7 0.0 copy-start.3
  88.7 0.0 all-reduce.2.cloned.1.call-update
  88.8 0.2 reduce-scatter.2.cloned.1.call-start
  89.0 0.6 copy-done.6
  89.6 0.1 copy.9
  89.7 59.3 %all-reduce.2.cloned.1.call-done.data_ref = f32[16,256,128]{2,1,0:T(8,128)} async-done(((f32[16,256,128]{2,1,0:T(8,128)}), f32[16,256,128]{2,1,0:T(8,128)}) %all-reduce.2.cloned.1.call-update) | async-done | bytes 2097168 | tf_op jit(solution)/shard_map/psum | solution.py:237
  149.1 0.0 copy-done.3
  149.1 0.0 copy-start.2
  149.1 1.6 copy-done.2
  150.6 27.0 %adjoint.1 = f32[4,16,32,256]{3,2,1,0:T(8,128)} custom-call(bf16[512,768]{1,0:T(8,128)(2,1)S(1)} %copy-done.1, bf16[1536,256]{1,0:T(8,128)(2,1)S(1)} %copy-done.3, f32[16,256,128]{2,1,0:T(8,128)S(1)} %copy-done.2, f32[256,128]{1,0:T(8,128)S(1)} %bitcast.8, bf16[256,2,128,256]{3,2,1,0:T(8,128)(2,1)} %kernel_transform.1.khat_ref), custom_call_target="tpu_custom_call" | custom-call | flops 1073741824 | bytes 33554432 | tf_op jit(solution)/shard_map/adjoint/pallas_call | solution.py:239
  177.7 0.0 copy-start.5
  177.7 0.0 copy-start.7
  177.7 0.0 reduce-scatter.2.cloned.1.call-update
  177.7 43.2 %reduce-scatter.2.cloned.1.call-done = f32[1,16,32,256]{3,2,1,0:T(8,128)} async-done(((f32[4,16,32,256]{3,2,1,0:T(8,128)}), f32[1,16,32,256]{3,2,1,0:T(8,128)}) %reduce-scatter.2.cloned.1.call-update) | async-done | bytes 524304 | tf_op jit(solution)/shard_map/reduce_scatter | solution.py:260
  220.9 0.0 copy-done.5
  220.9 0.0 copy-done.7
  220.9 1.4 bitcast_add_fusion
  222.3 1.1 copy.11
Async XLA Ops:
  6.5 51.1 %all-gather.3.cloned.1.call-start = ((), (), s32[]{:S(2)}) async-start(), calls=%async_computation.3 | async-start | bytes 2621440 | tf_op jit(solution)/shard_map/all_gather | solution.py:189
  7.3 141.8 %all-reduce.2.cloned.1.call-start = ((), (), s32[]{:S(2)}) async-start(), calls=%async_computation.1 | async-start | bytes 4194304 | tf_op jit(solution)/shard_map/psum | solution.py:237
  7.3 1.1 copy-start
  39.1 21.3 %copy-start.1 = (bf16[512,768]{1,0:T(8,128)(2,1)S(1)}, bf16[512,768]{1,0:T(8,128)(2,1)}, u32[]{:S(2)}) copy-start(bf16[512,768]{1,0:T(8,128)(2,1)} %constant.6.clone.table_ref) | copy-start | bytes 2359300
  39.2 21.3 %copy-start.4 = (bf16[256,1536]{1,0:T(8,128)(2,1)S(1)}, bf16[256,1536]{1,0:T(8,128)(2,1)}, u32[]{:S(2)}) copy-start(bf16[256,1536]{1,0:T(8,128)(2,1)} %constant.7.clone.inverse_ref) | copy-start | bytes 2359300
  88.7 0.9 copy-start.6
  88.7 60.3 %copy-start.3 = (bf16[1536,256]{1,0:T(8,128)(2,1)S(1)}, bf16[1536,256]{1,0:T(8,128)(2,1)}, u32[]{:S(2)}) copy-start(bf16[1536,256]{1,0:T(8,128)(2,1)} %constant.8.clone.inverse_ref) | copy-start | bytes 2359300
  88.8 132.2 %reduce-scatter.2.cloned.1.call-start = ((), (), s32[]{:S(2)}) async-start(), calls=%async_computation.2 | async-start | bytes 2621440 | tf_op jit(solution)/shard_map/reduce_scatter | solution.py:260
  149.1 1.6 copy-start.2
  177.7 43.3 %copy-start.5 = (f32[32,16,256]{2,1,0:T(8,128)S(1)}, f32[32,16,256]{2,1,0:T(8,128)}, u32[]{:S(2)}) copy-start(f32[32,16,256]{2,1,0:T(8,128)} %param.8) | copy-start | bytes 1572868
  177.7 43.3 %copy-start.7 = (f32[32]{0:T(128)S(1)}, f32[32]{0:T(128)}, u32[]{:S(2)}) copy-start(f32[32]{0:T(128)} %param.10) | copy-start | bytes 388
Sparse Core Ops, SparseCore 0:
  8.9 48.6 all-gather.2
  88.9 60.1 all-reduce.1
  177.8 43.0 reduce-scatter.1

commit v2 on v1

v2 whole, which is shorter than its diff:
```python
import functools
import math

import jax
import jax.numpy as jnp
import ml_dtypes
import numpy as np
from jax import lax
from jax.experimental import pallas as pl
from jax.experimental.pallas import tpu as pltpu
from jax.sharding import PartitionSpec as P

f32 = jnp.float32
bf16 = jnp.bfloat16
VMEM_LIMIT = 48 * 1024 * 1024
SENSOR_BLOCK = 16
FREQ_BLOCK = 16


def transform_table(steps):
    freqs = np.arange(steps, dtype=np.int64)[:, None]
    times = np.arange(steps, dtype=np.int64)[None, :]
    phase = ((2 * freqs + 1) * times % (4 * steps)).astype(np.float64) * (math.pi / (2 * steps))
    return np.concatenate([np.cos(phase), -np.sin(phase)], axis=0)


def split_host(table):
    table = table.astype(np.float32)
    high = table.astype(ml_dtypes.bfloat16)
    low = (table - high.astype(np.float32)).astype(ml_dtypes.bfloat16)
    return high, low


def split(value):
    high = value.astype(bf16)
    return high, (value - high.astype(f32)).astype(bf16)


def matmul(lhs, rhs):
    return lax.dot_general(lhs, rhs, (((1,), (0,)), ((), ())), preferred_element_type=f32)


def matmul_nt(lhs, rhs):
    return lax.dot_general(lhs, rhs, (((1,), (1,)), ((), ())), preferred_element_type=f32)


def kernel_transform(table_ref, kernel_ref, out_ref, real_ref, imag_ref):
    sensors, params, steps = kernel_ref.shape
    for s in range(0, sensors, 2):
        high, low = split(kernel_ref[s : s + 2].reshape(2 * params, steps))
        spec = matmul_nt(table_ref[...], jnp.concatenate([high, low, high], axis=1))
        for j in range(2):
            cols = slice(j * params, (j + 1) * params)
            real_ref[pl.ds(s + j, steps, stride=sensors), :] = spec[:steps, cols]
            imag_ref[pl.ds(s + j, steps, stride=sensors), :] = spec[steps:, cols]

    group = 8

    def emit(i, carry):
        rows = pl.ds(pl.multiple_of(i * group * sensors, group * sensors), group * sensors)
        freqs = pl.ds(i * group, group)
        for part, ref in enumerate((real_ref, imag_ref)):
            high, low = split(ref[rows, :].reshape(group, sensors, params))
            out_ref[freqs, 0, :, part * params : (part + 1) * params] = high
            out_ref[freqs, 1, :, part * params : (part + 1) * params] = low
        return carry

    lax.fori_loop(0, steps // group, emit, 0)


MESH = pl.DeviceIdType.MESH


def col_steps(bits):
    rest = list(range(1, bits))
    return [rest, rest[::-1]]


def normal_operator(
    bits,
    table_k_ref,
    inverse_t_ref,
    inverse_f_ref,
    hist_ref,
    noise_ref,
    khat_ref,
    out_ref,
    hreal_ref,
    himag_ref,
    spec_ref,
    grad_ref,
    time_ref,
    weighted_ref,
    *comm,
):
    recv_refs, (send_sem, recv_sem) = comm[:-2], comm[-2:]
    step = pl.program_id(0)
    half_steps = pl.num_programs(0) // 2
    blocks, vectors, part_params, steps = hist_ref.shape
    params = blocks * part_params
    freq_block, _, sensors, _ = khat_ref.shape
    total = vectors * steps
    me = lax.axis_index("col")
    bit_of = [lax.rem(me // 2**b, 2) for b in range(bits)]
    partner = [me + (1 - 2 * bit_of[b]) * 2**b for b in range(bits)]
    orders = col_steps(bits)

    @pl.when(step == 0)
    def _():
        barrier = pltpu.get_barrier_semaphore()
        for b in range(bits):
            pl.semaphore_signal(barrier, inc=1, device_id={"col": partner[b]}, device_id_type=MESH)
        pl.semaphore_wait(barrier, bits)

        for r in range(0, vectors, 2):
            hist = jnp.concatenate([hist_ref[:, r + j].reshape(params, steps) for j in range(2)], axis=0)
            high, low = split(hist)
            spec = matmul_nt(table_k_ref[...], jnp.concatenate([high, low, high], axis=1))
            for j in range(2):
                cols = slice(j * params, (j + 1) * params)
                hreal_ref[pl.ds(r + j, steps, stride=vectors), :] = spec[:steps, cols]
                himag_ref[pl.ds(r + j, steps, stride=vectors), :] = spec[steps:, cols]

    @pl.when(step < half_steps)
    def _():
        for i in range(freq_block):
            f = step * freq_block + i
            rows = pl.ds(pl.multiple_of(f * vectors, vectors), vectors)
            real, imag = hreal_ref[rows, :], himag_ref[rows, :]
            both = jnp.concatenate(
                [jnp.concatenate([real, -imag], axis=1), jnp.concatenate([imag, real], axis=1)], axis=0
            )
            lhs = jnp.concatenate(split(both), axis=0)
            res = matmul_nt(lhs, khat_ref[i].reshape(2 * sensors, 2 * params))
            top, bottom = res[: 2 * vectors], res[2 * vectors :]
            spec_ref[pl.ds(pl.multiple_of(f * 2 * vectors, 2 * vectors), 2 * vectors), :] = (
                top[:, :sensors] + (top[:, sensors:] + bottom[:, :sensors])
            )

    def to_time(r):
        spec = jnp.concatenate(
            [
                jnp.concatenate(
                    [spec_ref[pl.ds(part * vectors + r + j, steps, stride=2 * vectors), :] for j in range(2)],
                    axis=1,
                )
                for part in range(2)
            ],
            axis=0,
        )
        high, low = split(spec)
        times = matmul(inverse_t_ref[...], jnp.concatenate([high, low, high], axis=0))
        for j in range(2):
            rows = pl.ds(pl.multiple_of((r + j) * steps, steps), steps)
            time_ref[rows, :] = times[:, j * sensors : (j + 1) * sensors]

    def to_spectrum(r):
        rows = [pl.ds(pl.multiple_of((r + j) * steps, steps), steps) for j in range(2)]
        high, low = split(jnp.concatenate([weighted_ref[rows[j], :] for j in range(2)], axis=1))
        spec = matmul(table_k_ref[...], jnp.concatenate([high, low, high], axis=0))
        for j in range(2):
            cols = slice(j * sensors, (j + 1) * sensors)
            spec_ref[pl.ds(r + j, steps, stride=2 * vectors), :] = spec[:steps, cols]
            spec_ref[pl.ds(vectors + r + j, steps, stride=2 * vectors), :] = spec[steps:, cols]

    @pl.when(step == half_steps - 1)
    def _():
        def rows_of(offset, length):
            return pl.ds(pl.multiple_of(offset, 8), length)

        def exchange(src, dst, sem, bit):
            copy = pltpu.make_async_remote_copy(
                src_ref=src,
                dst_ref=dst,
                send_sem=send_sem.at[sem],
                recv_sem=recv_sem.at[sem],
                device_id={"col": partner[bit]},
                device_id_type=MESH,
            )
            copy.start()
            return copy

        half = vectors // 2
        keep, give = bit_of[0] * half, (1 - bit_of[0]) * half

        def give_body(j, carry):
            to_time(give + 2 * j)
            return carry

        def keep_body(j, carry):
            to_time(keep + 2 * j)
            return carry

        lax.fori_loop(0, half // 2, give_body, 0)
        length = total // 2
        first = exchange(time_ref.at[rows_of(give * steps, length)], recv_refs[0], 0, 0)
        lax.fori_loop(0, half // 2, keep_body, 0)
        first.wait()

        length //= 2
        offsets = [keep * steps, keep * steps + length]
        for part in range(2):
            rows = rows_of(offsets[part], length)
            time_ref[rows, :] += recv_refs[0][part * length : (part + 1) * length, :]
        sem = 1
        for level in range(bits - 1):
            length //= 2
            copies = []
            for part in range(2):
                bit = orders[part][level]
                send_at = offsets[part] + (1 - bit_of[bit]) * length
                offsets[part] = offsets[part] + bit_of[bit] * length
                copies.append(exchange(time_ref.at[rows_of(send_at, length)], recv_refs[sem], sem, bit))
                sem += 1
            for part in range(2):
                copies[part].wait()
                rows = rows_of(offsets[part], length)
                time_ref[rows, :] += recv_refs[sem - 2 + part][...]

        piece = min(length, steps)
        for part in range(2):
            for j in range(length // piece):
                at = offsets[part] + j * piece
                noise = noise_ref[rows_of(lax.rem(at, steps), piece), :]
                weighted_ref[rows_of(at, piece), :] = time_ref[rows_of(at, piece), :] * noise

        for level in reversed(range(bits - 1)):
            copies = []
            for part in range(2):
                bit = orders[part][level]
                rows = weighted_ref.at[rows_of(offsets[part], length)]
                copies.append(exchange(rows, rows, sem, bit))
                sem += 1
            for part in range(2):
                copies[part].wait()
                offsets[part] = offsets[part] - bit_of[orders[part][level]] * length
            length *= 2
        rows = weighted_ref.at[rows_of(keep * steps, 2 * length)]
        last = exchange(rows, rows, sem, 0)

        def keep_spectrum(j, carry):
            to_spectrum(keep + 2 * j)
            return carry

        def give_spectrum(j, carry):
            to_spectrum(give + 2 * j)
            return carry

        lax.fori_loop(0, half // 2, keep_spectrum, 0)
        last.wait()
        lax.fori_loop(0, half // 2, give_spectrum, 0)

    @pl.when(step >= half_steps)
    def _():
        for i in range(freq_block):
            f = (step - half_steps) * freq_block + i
            base = pl.multiple_of(f * 2 * vectors, 2 * vectors)
            high, low = split(spec_ref[pl.ds(base, 2 * vectors), :])
            lhs = jnp.concatenate(
                [jnp.concatenate([high, high], axis=1), jnp.concatenate([low, jnp.zeros_like(low)], axis=1)], axis=0
            )
            res = matmul(lhs, khat_ref[i].reshape(2 * sensors, 2 * params))
            res = res[: 2 * vectors] + res[2 * vectors :]
            grad_ref[pl.ds(base, vectors), :] = res[:vectors, :params] + res[vectors:, params:]
            grad_ref[pl.ds(base + vectors, vectors), :] = res[vectors:, :params] - res[:vectors, params:]

    @pl.when(step == 2 * half_steps - 1)
    def _():
        for r in range(0, vectors, 2):
            spec = jnp.concatenate(
                [
                    jnp.concatenate(
                        [grad_ref[pl.ds(part * vectors + r + j, steps, stride=2 * vectors), :] for part in range(2)],
                        axis=0,
                    ).T
                    for j in range(2)
                ],
                axis=0,
            )
            high, low = split(spec)
            times = matmul(jnp.concatenate([high, low, high], axis=1), inverse_f_ref[...])
            for j in range(2):
                out_ref[:, r + j] = times[j * params : (j + 1) * params].reshape(blocks, part_params, steps)


def local(col_count, row_count, kernel, history, noise_weight, prior_weight):
    sensors, params, steps = kernel.shape
    part_params, vectors, _ = history.shape
    pad = -sensors % 128
    if pad:
        kernel = jnp.pad(kernel, ((0, pad), (0, 0), (0, 0)))
        noise_weight = jnp.pad(noise_weight, ((0, pad), (0, 0)))
        sensors += pad

    table = transform_table(steps)
    th, tl = split_host(table)
    ih, il = split_host(table / steps)
    table_k = jnp.asarray(np.concatenate([th, th, tl], axis=1))
    inverse_t = jnp.asarray(np.concatenate([ih.T, ih.T, il.T], axis=1))
    inverse_f = jnp.asarray(np.concatenate([ih, ih, il], axis=0))

    whole = lambda *shape: pl.BlockSpec(shape, lambda i: (0,) * len(shape))
    params_of = pltpu.CompilerParams(vmem_limit_bytes=VMEM_LIMIT)

    moved = history.transpose(1, 0, 2)
    gathered = lax.all_gather(moved, "row", axis=0)

    khat = pl.pallas_call(
        kernel_transform,
        grid=(sensors // SENSOR_BLOCK,),
        in_specs=[
            whole(2 * steps, 3 * steps),
            pl.BlockSpec((SENSOR_BLOCK, params, steps), lambda i: (i, 0, 0)),
        ],
        out_specs=pl.BlockSpec((steps, 2, SENSOR_BLOCK, 2 * params), lambda i: (0, 0, i, 0)),
        out_shape=jax.ShapeDtypeStruct((steps, 2, sensors, 2 * params), bf16),
        scratch_shapes=[pltpu.VMEM((steps * SENSOR_BLOCK, params), f32)] * 2,
        compiler_params=params_of,
        cost_estimate=pl.CostEstimate(
            flops=12 * sensors * params * steps * steps,
            bytes_accessed=12 * sensors * params * steps,
            transcendentals=0,
        ),
        name="kernel_transform",
    )(table_k, kernel)

    bits = col_count.bit_length() - 1
    total = vectors * steps
    lengths = [total // 2]
    for level in range(bits - 1):
        lengths += [total >> (level + 3)] * 2
    half_steps = steps // FREQ_BLOCK
    grad = pl.pallas_call(
        functools.partial(normal_operator, bits),
        grid=(2 * half_steps,),
        in_specs=[
            whole(2 * steps, 3 * steps),
            whole(steps, 6 * steps),
            whole(6 * steps, steps),
            whole(row_count, vectors, part_params, steps),
            whole(steps, sensors),
            pl.BlockSpec((FREQ_BLOCK, 2, sensors, 2 * params), lambda i: (lax.rem(i, half_steps), 0, 0, 0)),
        ],
        out_specs=whole(row_count, vectors, part_params, steps),
        out_shape=jax.ShapeDtypeStruct((row_count, vectors, part_params, steps), f32),
        scratch_shapes=[
            pltpu.VMEM((steps * vectors, params), f32),
            pltpu.VMEM((steps * vectors, params), f32),
            pltpu.VMEM((steps * 2 * vectors, sensors), f32),
            pltpu.VMEM((steps * 2 * vectors, params), f32),
            pltpu.VMEM((total, sensors), f32),
            pltpu.VMEM((total, sensors), f32),
            *[pltpu.VMEM((length, sensors), f32) for length in lengths],
            pltpu.SemaphoreType.DMA((2 * len(lengths),)),
            pltpu.SemaphoreType.DMA((2 * len(lengths),)),
        ],
        compiler_params=pltpu.CompilerParams(
            vmem_limit_bytes=VMEM_LIMIT, collective_id=0, has_side_effects=True
        ),
        cost_estimate=pl.CostEstimate(
            flops=32 * vectors * sensors * params * steps,
            bytes_accessed=16 * sensors * params * steps,
            transcendentals=0,
        ),
        name="normal_operator",
    )(table_k, inverse_t, inverse_f, gathered, noise_weight.T, khat)

    gradient = lax.psum_scatter(grad, "row", scatter_dimension=0, tiled=False)
    return gradient.transpose(1, 0, 2) + prior_weight[:, None, None] * history


def solution(mesh):
    in_specs = (
        P("row", "col", None),
        P(("col", "row"), None, None),
        P("row", None),
        P(("col", "row")),
    )
    out_specs = P(("col", "row"), None, None)
    return jax.shard_map(
        functools.partial(local, mesh.shape["col"], mesh.shape["row"]),
        mesh=mesh,
        in_specs=in_specs,
        out_specs=out_specs,
        check_vma=False,
    )
```

time: 231 us -> 194 us (0.84)
  waiting for transfers between devices: 122 us -> 60.1 us
  Pallas kernels: 86 us -> 111 us
    psum x1 -> x0, waiting for transfers between devices: 59.3 us -> none  [local(): data = lax.psum(partial, 'col')]
    pallas_call x2 -> x1, Pallas kernels: 55.3 us -> 80.4 us  [local(): pl.pallas_call(functools.partial(normal_operator, bits), grid=(2 * half_s...]
  transfers between devices with their start and end apart: 3 -> 2, of which waited for: 3 -> 2; matrix products, arithmetic and copies ran while one was open for 0% -> 1% of each run, Pallas kernels for 13% -> 16%
where the time goes in v2:
time: 194 us; the launch traced here: 193 us
  Pallas kernels  111 us (57%)
  waiting for transfers between devices  60.1 us (31%)
  between operations  13.5 us (7%)
  local copies, waits for them, and re-layouts  7.4 us (4%)
    pallas_call x1, Pallas kernels, local(): pl.pallas_call(functools.partial(normal_operator, bits), grid=(2 * half_s...  80.4 us
    reduce_scatter x1, waiting for transfers between devices, local(): gradient = lax.psum_scatter(grad, 'row', scatter_dimension=0, tiled=False)  41.9 us
    pallas_call x1, Pallas kernels, local(): pl.pallas_call(kernel_transform, grid=(sensors // SENSOR_BLOCK,), in_spec...  30.7 us
    all_gather x1, waiting for transfers between devices, local(): gathered = lax.all_gather(moved, 'row', axis=0)  17.5 us
    all_gather x1, local copies, waits for them, and re-layouts, local(): gathered = lax.all_gather(moved, 'row', axis=0)  4.15 us
  transfers between devices with their start and end apart: 2, of which 2 were waited for; matrix products, arithmetic and copies ran while one was open for 1% of the time, Pallas kernels for 16%

profile of v2, /device:TPU:0, one launch (start us, length us, event | category | flops | bytes accessed | tf_op | source)
XLA Modules:
  0.0 193.4 jit_solution(15569356519545375702)
XLA Ops:
  6.5 0.0 all-gather.3.cloned.1.call-start
  6.5 0.7 all-gather.3.cloned.1.call-update
  7.3 0.0 reduce-scatter.2.cloned.1.call-start
  7.3 1.0 copy.9
  8.3 0.0 copy-start
  8.3 1.1 copy-done
  9.4 30.7 %kernel_transform.1.khat_ref = bf16[256,2,128,256]{3,2,1,0:T(8,128)(2,1)} custom-call(bf16[512,768]{1,0:T(8,128)(2,1)S(1)} %copy-done, f32[128,128,256]{2,1,0:T(8,128)} %kernel_ref.1), custom_call_target="tpu_custom_call" | custom-call | flops 12884901888 | bytes 50331648 | tf_op jit(solution)/shard_map/kernel_transform/pallas_call | solution.py:308
  40.1 0.0 copy-start.1
  40.1 0.0 copy-start.2
  40.1 0.0 copy-start.3
  40.1 17.5 %all-gather.3.cloned.1.call-done = f32[64,32,256]{2,0,1:T(8,128)} async-done(((f32[16,32,256]{2,0,1:T(8,128)}), f32[64,32,256]{2,0,1:T(8,128)}) %all-gather.3.cloned.1.call-update) | async-done | bytes 2097168 | tf_op jit(solution)/shard_map/all_gather | solution.py:306
  57.6 4.2 %copy.8 = f32[64,32,256]{2,1,0:T(8,128)} copy(f32[64,32,256]{2,0,1:T(8,128)} %all-gather.3.cloned.1.call-done) | data formatting | bytes 4194304 | tf_op jit(solution)/shard_map/all_gather | solution.py:306
  61.8 0.0 copy-done.1
  61.8 0.0 copy-done.2
  61.8 0.0 copy-done.3
  61.8 80.4 %normal_operator.1 = f32[4,16,32,256]{3,2,1,0:T(8,128)} custom-call(bf16[512,768]{1,0:T(8,128)(2,1)S(1)} %copy-done.1, bf16[256,1536]{1,0:T(8,128)(2,1)S(1)} %copy-done.3, bf16[1536,256]{1,0:T(8,128)(2,1)S(1)} %copy-done.2, f32[4,16,32,256]{3,2,1,0:T(8,128)} %bitcast.8, f32[256,128]{1,0:T(8,128)S(1)} %bitcast.7, ...), custom_call_target="tpu_custom_call" | custom-call | flops 2147483648 | bytes 67108864 | tf_op jit(solution)/shard_map/normal_operator/pallas_call | solution.py:333
  142.2 0.0 copy-start.4
  142.2 0.0 copy-start.5
  142.2 0.0 reduce-scatter.2.cloned.1.call-update
  142.2 41.9 %reduce-scatter.2.cloned.1.call-done = f32[1,16,32,256]{3,2,1,0:T(8,128)} async-done(((f32[4,16,32,256]{3,2,1,0:T(8,128)}), f32[1,16,32,256]{3,2,1,0:T(8,128)}) %reduce-scatter.2.cloned.1.call-update) | async-done | bytes 524304 | tf_op jit(solution)/shard_map/reduce_scatter | solution.py:368
  184.1 0.0 copy-done.4
  184.1 0.0 copy-done.5
  184.1 1.4 bitcast_add_fusion
  185.5 1.1 copy.11
Async XLA Ops:
  6.5 51.1 %all-gather.3.cloned.1.call-start = ((), (), s32[]{:S(2)}) async-start(), calls=%async_computation.2 | async-start | bytes 2621440 | tf_op jit(solution)/shard_map/all_gather | solution.py:306
  7.3 176.8 %reduce-scatter.2.cloned.1.call-start = ((), (), s32[]{:S(2)}) async-start(), calls=%async_computation.1 | async-start | bytes 2621440 | tf_op jit(solution)/shard_map/reduce_scatter | solution.py:368
  8.3 1.1 copy-start
  40.1 21.7 %copy-start.1 = (bf16[512,768]{1,0:T(8,128)(2,1)S(1)}, bf16[512,768]{1,0:T(8,128)(2,1)}, u32[]{:S(2)}) copy-start(bf16[512,768]{1,0:T(8,128)(2,1)} %constant.6.clone.table_ref.table_k_ref) | copy-start | bytes 2359300
  40.1 21.7 %copy-start.2 = (bf16[1536,256]{1,0:T(8,128)(2,1)S(1)}, bf16[1536,256]{1,0:T(8,128)(2,1)}, u32[]{:S(2)}) copy-start(bf16[1536,256]{1,0:T(8,128)(2,1)} %constant.8.clone.inverse_f_ref) | copy-start | bytes 2359300
  40.1 21.7 %copy-start.3 = (bf16[256,1536]{1,0:T(8,128)(2,1)S(1)}, bf16[256,1536]{1,0:T(8,128)(2,1)}, u32[]{:S(2)}) copy-start(bf16[256,1536]{1,0:T(8,128)(2,1)} %constant.7.clone.inverse_t_ref) | copy-start | bytes 2359300
  142.2 41.9 %copy-start.4 = (f32[32,16,256]{2,1,0:T(8,128)S(1)}, f32[32,16,256]{2,1,0:T(8,128)}, u32[]{:S(2)}) copy-start(f32[32,16,256]{2,1,0:T(8,128)} %param.8) | copy-start | bytes 1572868
  142.2 41.9 %copy-start.5 = (f32[32]{0:T(128)S(1)}, f32[32]{0:T(128)}, u32[]{:S(2)}) copy-start(f32[32]{0:T(128)} %param.10) | copy-start | bytes 388
Sparse Core Ops, SparseCore 0:
  8.9 48.6 all-gather.2
  142.3 41.6 reduce-scatter.1

commit v3 on v2

--- a/solution.py
+++ b/solution.py
@@ -44,8 +44,106 @@
     return lax.dot_general(lhs, rhs, (((1,), (1,)), ((), ())), preferred_element_type=f32)
 
 
-def kernel_transform(table_ref, kernel_ref, out_ref, real_ref, imag_ref):
+MESH = pl.DeviceIdType.MESH
+CHUNKS = 2
+
+
+def greet_row(me, last, others=0):
+    barrier = pltpu.get_barrier_semaphore()
+
+    @pl.when(me > 0)
+    def _():
+        pl.semaphore_signal(barrier, inc=1, device_id={"row": me - 1}, device_id_type=MESH)
+
+    @pl.when(me < last)
+    def _():
+        pl.semaphore_signal(barrier, inc=1, device_id={"row": me + 1}, device_id_type=MESH)
+
+    inside = (me > 0) & (me < last)
+
+    @pl.when(inside)
+    def _():
+        pl.semaphore_wait(barrier, others + 2)
+
+    @pl.when(jnp.logical_not(inside))
+    def _():
+        pl.semaphore_wait(barrier, others + 1)
+
+
+def kernel_transform(
+    row_count, table_ref, kernel_ref, hist_ref, out_ref, all_ref, real_ref, imag_ref, own_sem, right_sems, left_sems
+):
     sensors, params, steps = kernel_ref.shape
+    grid_step = pl.program_id(0)
+    grid_steps = pl.num_programs(0)
+    me = lax.axis_index("row")
+    last = row_count - 1
+    half = hist_ref.shape[0] // CHUNKS
+    own = pltpu.make_async_copy(hist_ref, all_ref.at[me], own_sem)
+
+    def hop(h, c, right):
+        shard = me - h if right else me + h
+        sems = right_sems if right else left_sems
+        rows = pl.ds(c * half, half)
+        slot = all_ref.at[shard, rows]
+        return pltpu.make_async_remote_copy(
+            src_ref=hist_ref.at[rows] if h == 0 else slot,
+            dst_ref=slot,
+            send_sem=sems.at[0, h * CHUNKS + c],
+            recv_sem=sems.at[1, h * CHUNKS + c],
+            device_id={"row": me + 1 if right else me - 1},
+            device_id_type=MESH,
+        )
+
+    def sends(h, right):
+        return (me < last) & (me >= h) if right else (me > 0) & (me <= last - h)
+
+    def receives(h, right):
+        return me >= h + 1 if right else me <= last - h - 1
+
+    def arrival(h, c, right):
+        rows = pl.ds(c * half, half)
+        slot = all_ref.at[me - 1 - h if right else me + 1 + h, rows]
+        sems = right_sems if right else left_sems
+        return pltpu.make_async_remote_copy(
+            src_ref=slot,
+            dst_ref=slot,
+            send_sem=sems.at[0, h * CHUNKS + c],
+            recv_sem=sems.at[1, h * CHUNKS + c],
+            device_id={"row": me - 1 if right else me + 1},
+            device_id_type=MESH,
+        )
+
+    def wait_arrival(h, c):
+        for right in (True, False):
+
+            @pl.when(receives(h, right))
+            def _():
+                arrival(h, c, right).wait_recv()
+
+    def start_hop(h, c):
+        for right in (True, False):
+
+            @pl.when(sends(h, right))
+            def _():
+                hop(h, c, right).start()
+
+    @pl.when(grid_step == 0)
+    def _():
+        greet_row(me, last)
+        for c in range(CHUNKS):
+            start_hop(0, c)
+        own.start()
+
+    for m in range(CHUNKS * (row_count - 2)):
+        h, c = m // CHUNKS, m % CHUNKS
+        due = jnp.minimum((m + 1) * grid_steps // (CHUNKS * last) + 1, grid_steps - 1)
+
+        @pl.when(grid_step == due)
+        def _():
+            wait_arrival(h, c)
+            start_hop(h + 1, c)
+
     for s in range(0, sensors, 2):
         high, low = split(kernel_ref[s : s + 2].reshape(2 * params, steps))
         spec = matmul_nt(table_ref[...], jnp.concatenate([high, low, high], axis=1))
@@ -67,8 +165,18 @@
 
     lax.fori_loop(0, steps // group, emit, 0)
 
-
-MESH = pl.DeviceIdType.MESH
+    @pl.when(grid_step == grid_steps - 1)
+    def _():
+        own.wait()
+        for c in range(CHUNKS):
+            wait_arrival(row_count - 2, c)
+        for h in range(row_count - 1):
+            for c in range(CHUNKS):
+                for right in (True, False):
+
+                    @pl.when(sends(h, right))
+                    def _():
+                        hop(h, c, right).wait_send()
 
 
 def col_steps(bits):
@@ -91,9 +199,12 @@
     grad_ref,
     time_ref,
     weighted_ref,
+    partial_ref,
+    from_left_ref,
+    from_right_ref,
     *comm,
 ):
-    recv_refs, (send_sem, recv_sem) = comm[:-2], comm[-2:]
+    recv_refs, (send_sem, recv_sem, right_sems, left_sems) = comm[:-4], comm[-4:]
     step = pl.program_id(0)
     half_steps = pl.num_programs(0) // 2
     blocks, vectors, part_params, steps = hist_ref.shape
@@ -110,7 +221,7 @@
         barrier = pltpu.get_barrier_semaphore()
         for b in range(bits):
             pl.semaphore_signal(barrier, inc=1, device_id={"col": partner[b]}, device_id_type=MESH)
-        pl.semaphore_wait(barrier, bits)
+        greet_row(lax.axis_index("row"), blocks - 1, bits)
 
         for r in range(0, vectors, 2):
             hist = jnp.concatenate([hist_ref[:, r + j].reshape(params, steps) for j in range(2)], axis=0)
@@ -266,7 +377,11 @@
 
     @pl.when(step == 2 * half_steps - 1)
     def _():
-        for r in range(0, vectors, 2):
+        chunk = vectors // CHUNKS
+        last = blocks - 1
+        row = lax.axis_index("row")
+
+        def to_gradient(r):
             spec = jnp.concatenate(
                 [
                     jnp.concatenate(
@@ -280,7 +395,66 @@
             high, low = split(spec)
             times = matmul(jnp.concatenate([high, low, high], axis=1), inverse_f_ref[...])
             for j in range(2):
-                out_ref[:, r + j] = times[j * params : (j + 1) * params].reshape(blocks, part_params, steps)
+                partial_ref[:, r + j] = times[j * params : (j + 1) * params].reshape(blocks, part_params, steps)
+
+        def turn(q, c, right, arriving=False):
+            rows = pl.ds(c * chunk, chunk)
+            sems = right_sems if right else left_sems
+            landing = from_left_ref if right else from_right_ref
+            return pltpu.make_async_remote_copy(
+                src_ref=partial_ref.at[last - q if right else q, rows],
+                dst_ref=landing.at[q, rows],
+                send_sem=sems.at[0, q * CHUNKS + c],
+                recv_sem=sems.at[1, q * CHUNKS + c],
+                device_id={"row": row + 1 if right != arriving else row - 1},
+                device_id_type=MESH,
+            )
+
+        def step_of_line(t, c):
+            rows = pl.ds(c * chunk, chunk)
+            for right in (True, False):
+                behind = row if right else last - row
+                q = t - behind
+                landing = from_left_ref if right else from_right_ref
+
+                @pl.when((q >= 0) & (q <= last - behind) & (behind > 0))
+                def _():
+                    turn(q, c, right, arriving=True).wait_recv()
+                    shard = last - q if right else q
+                    partial_ref[shard, rows] += landing[q, rows]
+
+                @pl.when((q >= 0) & (q < last - behind))
+                def _():
+                    @pl.when(q >= 1)
+                    def _():
+                        turn(q - 1, c, right).wait_send()
+
+                    turn(q, c, right).start()
+
+        for c in range(CHUNKS):
+
+            def gradient_body(j, carry):
+                to_gradient(c * chunk + 2 * j)
+                return carry
+
+            lax.fori_loop(0, chunk // 2, gradient_body, 0)
+            step_of_line(0, c)
+
+        def line_body(t, carry):
+            for c in range(CHUNKS):
+                step_of_line(t, c)
+            return carry
+
+        lax.fori_loop(1, blocks, line_body, 0)
+        out_ref[...] = partial_ref[row]
+
+        for right in (True, False):
+            behind = row if right else last - row
+
+            @pl.when(behind < last)
+            def _():
+                for c in range(CHUNKS):
+                    turn(last - behind - 1, c, right).wait_send()
 
 
 def local(col_count, row_count, kernel, history, noise_weight, prior_weight):
@@ -300,29 +474,43 @@
     inverse_f = jnp.asarray(np.concatenate([ih, ih, il], axis=0))
 
     whole = lambda *shape: pl.BlockSpec(shape, lambda i: (0,) * len(shape))
-    params_of = pltpu.CompilerParams(vmem_limit_bytes=VMEM_LIMIT)
 
     moved = history.transpose(1, 0, 2)
-    gathered = lax.all_gather(moved, "row", axis=0)
-
-    khat = pl.pallas_call(
-        kernel_transform,
+    hops = CHUNKS * (row_count - 1)
+    anywhere = pl.BlockSpec(memory_space=pl.ANY)
+    khat, gathered = pl.pallas_call(
+        functools.partial(kernel_transform, row_count),
         grid=(sensors // SENSOR_BLOCK,),
         in_specs=[
             whole(2 * steps, 3 * steps),
             pl.BlockSpec((SENSOR_BLOCK, params, steps), lambda i: (i, 0, 0)),
+            anywhere,
         ],
-        out_specs=pl.BlockSpec((steps, 2, SENSOR_BLOCK, 2 * params), lambda i: (0, 0, i, 0)),
-        out_shape=jax.ShapeDtypeStruct((steps, 2, sensors, 2 * params), bf16),
-        scratch_shapes=[pltpu.VMEM((steps * SENSOR_BLOCK, params), f32)] * 2,
-        compiler_params=params_of,
+        out_specs=[
+            pl.BlockSpec((steps, 2, SENSOR_BLOCK, 2 * params), lambda i: (0, 0, i, 0)),
+            anywhere,
+        ],
+        out_shape=[
+            jax.ShapeDtypeStruct((steps, 2, sensors, 2 * params), bf16),
+            jax.ShapeDtypeStruct((row_count, vectors, part_params, steps), f32),
+        ],
+        scratch_shapes=[
+            pltpu.VMEM((steps * SENSOR_BLOCK, params), f32),
+            pltpu.VMEM((steps * SENSOR_BLOCK, params), f32),
+            pltpu.SemaphoreType.DMA,
+            pltpu.SemaphoreType.DMA((2, hops)),
+            pltpu.SemaphoreType.DMA((2, hops)),
+        ],
+        compiler_params=pltpu.CompilerParams(
+            vmem_limit_bytes=VMEM_LIMIT, collective_id=1, has_side_effects=True
+        ),
         cost_estimate=pl.CostEstimate(
             flops=12 * sensors * params * steps * steps,
             bytes_accessed=12 * sensors * params * steps,
             transcendentals=0,
         ),
         name="kernel_transform",
-    )(table_k, kernel)
+    )(table_k, kernel, moved)
 
     bits = col_count.bit_length() - 1
     total = vectors * steps
@@ -330,7 +518,7 @@
     for level in range(bits - 1):
         lengths += [total >> (level + 3)] * 2
     half_steps = steps // FREQ_BLOCK
-    grad = pl.pallas_call(
+    gradient = pl.pallas_call(
         functools.partial(normal_operator, bits),
         grid=(2 * half_steps,),
         in_specs=[
@@ -341,8 +529,8 @@
             whole(steps, sensors),
             pl.BlockSpec((FREQ_BLOCK, 2, sensors, 2 * params), lambda i: (lax.rem(i, half_steps), 0, 0, 0)),
         ],
-        out_specs=whole(row_count, vectors, part_params, steps),
-        out_shape=jax.ShapeDtypeStruct((row_count, vectors, part_params, steps), f32),
+        out_specs=whole(vectors, part_params, steps),
+        out_shape=jax.ShapeDtypeStruct((vectors, part_params, steps), f32),
         scratch_shapes=[
             pltpu.VMEM((steps * vectors, params), f32),
             pltpu.VMEM((steps * vectors, params), f32),
@@ -350,9 +538,14 @@
             pltpu.VMEM((steps * 2 * vectors, params), f32),
             pltpu.VMEM((total, sensors), f32),
             pltpu.VMEM((total, sensors), f32),
+            pltpu.VMEM((row_count, vectors, part_params, steps), f32),
+            pltpu.VMEM((row_count - 1, vectors, part_params, steps), f32),
+            pltpu.VMEM((row_count - 1, vectors, part_params, steps), f32),
             *[pltpu.VMEM((length, sensors), f32) for length in lengths],
             pltpu.SemaphoreType.DMA((2 * len(lengths),)),
             pltpu.SemaphoreType.DMA((2 * len(lengths),)),
+            pltpu.SemaphoreType.DMA((2, hops)),
+            pltpu.SemaphoreType.DMA((2, hops)),
         ],
         compiler_params=pltpu.CompilerParams(
             vmem_limit_bytes=VMEM_LIMIT, collective_id=0, has_side_effects=True
@@ -365,7 +558,6 @@
         name="normal_operator",
     )(table_k, inverse_t, inverse_f, gathered, noise_weight.T, khat)
 
-    gradient = lax.psum_scatter(grad, "row", scatter_dimension=0, tiled=False)
     return gradient.transpose(1, 0, 2) + prior_weight[:, None, None] * history
 
 

time: 194 us -> 162 us (0.84)
  waiting for transfers between devices: 60.1 us -> 0 us
  Pallas kernels: 111 us -> 155 us
  between operations: 13.5 us -> 0.08 us
    reduce_scatter x1 -> x0, waiting for transfers between devices: 41.9 us -> none  [local(): gradient = lax.psum_scatter(grad, 'row', scatter_dimension=0, tiled=False)]
    pallas_call x1, Pallas kernels: 80.4 us -> 113 us  [local(): pl.pallas_call(functools.partial(normal_operator, bits), grid=(2 * half_s...]
    all_gather x1 -> x0, waiting for transfers between devices: 17.5 us -> none  [local(): gathered = lax.all_gather(moved, 'row', axis=0)]
    pallas_call x1, Pallas kernels: 30.7 us -> 42.7 us  [local(): pl.pallas_call(functools.partial(kernel_transform, row_count), grid=(sens...]
    all_gather x1 -> x0, local copies, waits for them, and re-layouts: 4.15 us -> none  [local(): gathered = lax.all_gather(moved, 'row', axis=0)]
    unnamed x13 -> x16, local copies, waits for them, and re-layouts: 2.15 us -> 4.84 us
  transfers between devices with their start and end apart: 2 -> 0, of which waited for: 2 -> 0; matrix products, arithmetic and copies ran while one was open for 1% -> 0% of each run, Pallas kernels for 16% -> 0%
where the time goes in v3:
time: 162 us
  Pallas kernels  155 us (96%)
  local copies, waits for them, and re-layouts  5.94 us (4%)
    pallas_call x1, Pallas kernels, local(): pl.pallas_call(functools.partial(normal_operator, bits), grid=(2 * half_s...  113 us
    pallas_call x1, Pallas kernels, local(): pl.pallas_call(functools.partial(kernel_transform, row_count), grid=(sens...  42.7 us
    unnamed x16, local copies, waits for them, and re-layouts  4.84 us

profile of v3, /device:TPU:0, one launch (start us, length us, event | category | flops | bytes accessed | tf_op | source)
XLA Modules:
  0.0 161.7 jit_solution(3664378626274892424)
XLA Ops:
  0.0 1.3 copy.14
  1.4 0.0 copy-start
  1.4 1.1 copy-done
  2.5 0.0 copy-start.5
  2.5 0.0 copy-start.1
  2.5 42.7 %kernel_transform.1 = (bf16[256,2,128,256]{3,2,1,0:T(8,128)(2,1)}, f32[4,16,32,256]{3,2,1,0:T(8,128)S(1)}) custom-call(bf16[512,768]{1,0:T(8,128)(2,1)S(1)} %copy-done, f32[128,128,256]{2,1,0:T(8,128)} %kernel_ref.1, f32[16,32,256]{2,1,0:T(8,128)S(1)} %bitcast.7), custom_call_target="tpu_custom_call" | custom-call | flops 12884901888 | bytes 50331648 | tf_op jit(solution)/shard_map/kernel_transform/pallas_call | solution.py:481
  45.2 0.0 copy-done.5
  45.2 0.1 copy.9
  45.3 0.0 copy-done.1
  45.3 0.0 copy-start.2
  45.3 1.1 copy-done.2
  46.4 0.0 copy-start.3
  46.4 1.1 copy-done.3
  47.5 0.0 copy-start.4
  47.5 0.0 copy-start.6
  47.5 112.7 %normal_operator.1 = f32[16,32,256]{2,1,0:T(8,128)S(1)} custom-call(bf16[512,768]{1,0:T(8,128)(2,1)S(1)} %copy-done.1, bf16[256,1536]{1,0:T(8,128)(2,1)S(1)} %copy-done.2, bf16[1536,256]{1,0:T(8,128)(2,1)S(1)} %copy-done.3, f32[4,16,32,256]{3,2,1,0:T(8,128)S(1)} %get-tuple-element.7.hist_ref, f32[256,128]{1,0:T(8,128)S(1)} %bitcast.6, ...), custom_call_target="tpu_custom_call" | custom-call | flops 2147483648 | bytes 67108864 | tf_op jit(solution)/shard_map/normal_operator/pallas_call | solution.py:521
  160.2 0.0 copy-done.4
  160.2 0.0 copy-done.6
  160.3 0.3 bitcast_add_fusion
  160.6 1.1 copy.11
Async XLA Ops:
  1.4 1.1 copy-start
  2.5 42.7 %copy-start.5 = (f32[128,256]{1,0:T(8,128)S(1)}, f32[128,256]{1,0:T(8,128)}, u32[]{:S(2)}) copy-start(f32[128,256]{1,0:T(8,128)} %param.9) | copy-start | bytes 393220
  2.5 42.8 %copy-start.1 = (bf16[512,768]{1,0:T(8,128)(2,1)S(1)}, bf16[512,768]{1,0:T(8,128)(2,1)}, u32[]{:S(2)}) copy-start(bf16[512,768]{1,0:T(8,128)(2,1)} %constant.6.clone.table_ref.table_k_ref) | copy-start | bytes 2359300
  45.3 1.1 copy-start.2
  46.4 1.1 copy-start.3
  47.5 112.7 %copy-start.4 = (f32[32,16,256]{2,1,0:T(8,128)S(1)}, f32[32,16,256]{2,1,0:T(8,128)}, u32[]{:S(2)}) copy-start(f32[32,16,256]{2,1,0:T(8,128)} %param.8) | copy-start | bytes 1572868
  47.5 112.7 %copy-start.6 = (f32[32]{0:T(128)S(1)}, f32[32]{0:T(128)}, u32[]{:S(2)}) copy-start(f32[32]{0:T(128)} %param.10) | copy-start | bytes 388

commit v4 on v3

--- a/solution.py
+++ b/solution.py
@@ -12,9 +12,9 @@
 
 f32 = jnp.float32
 bf16 = jnp.bfloat16
-VMEM_LIMIT = 48 * 1024 * 1024
+VMEM_LIMIT = 60 * 1024 * 1024
 SENSOR_BLOCK = 16
-FREQ_BLOCK = 16
+FREQ_BLOCK = 32
 
 
 def transform_table(steps):
@@ -159,8 +159,8 @@
         freqs = pl.ds(i * group, group)
         for part, ref in enumerate((real_ref, imag_ref)):
             high, low = split(ref[rows, :].reshape(group, sensors, params))
-            out_ref[freqs, 0, :, part * params : (part + 1) * params] = high
-            out_ref[freqs, 1, :, part * params : (part + 1) * params] = low
+            out_ref[freqs, 0, 0, :, part * params : (part + 1) * params] = high
+            out_ref[freqs, 0, 1, :, part * params : (part + 1) * params] = low
         return carry
 
     lax.fori_loop(0, steps // group, emit, 0)
@@ -184,43 +184,144 @@
     return [rest, rest[::-1]]
 
 
+def rows_of(offset, length):
+    return pl.ds(pl.multiple_of(offset, 8), length)
+
+
+class AllReduce:
+    def __init__(self, bits, half_sensors, time_ref, weighted_ref, noise_ref, recv_refs, send_sem, recv_sem):
+        me = lax.axis_index("col")
+        self.bits, self.steps = bits, noise_ref.shape[0]
+        self.time_ref, self.weighted_ref, self.noise_ref = time_ref, weighted_ref, noise_ref
+        self.recv_refs, self.send_sem, self.recv_sem = recv_refs, send_sem, recv_sem
+        self.bit_of = [lax.rem(me // 2**b, 2) for b in range(bits)]
+        self.partner = [me + (1 - 2 * self.bit_of[b]) * 2**b for b in range(bits)]
+        self.orders = col_steps(bits)
+        total = time_ref.shape[0]
+        self.core_length = total // 2
+        self.keep = self.bit_of[0] * self.core_length
+        self.give = (1 - self.bit_of[0]) * self.core_length
+        length = self.core_length // 2
+        self.offsets = [[self.keep, self.keep + length]]
+        self.lengths = [length]
+        for level in range(bits - 1):
+            length //= 2
+            self.lengths.append(length)
+            self.offsets.append(
+                [
+                    self.offsets[-1][part] + self.bit_of[self.orders[part][level]] * length
+                    for part in range(2)
+                ]
+            )
+
+    def copy(self, src, dst, sem, bit):
+        return pltpu.make_async_remote_copy(
+            src_ref=src,
+            dst_ref=dst,
+            send_sem=self.send_sem.at[sem],
+            recv_sem=self.recv_sem.at[sem],
+            device_id={"col": self.partner[bit]},
+            device_id_type=MESH,
+        )
+
+    def stage(self, k):
+        levels = self.bits - 1
+        if k == 0:
+            return [self.copy(self.time_ref.at[rows_of(self.give, self.core_length)], self.recv_refs[0], 0, 0)]
+        if k == 2 * levels + 1:
+            rows = self.weighted_ref.at[rows_of(self.keep, self.core_length)]
+            return [self.copy(rows, rows, 4 * levels + 1, 0)]
+        copies = []
+        for part in range(2):
+            sem = 2 * k - 1 + part
+            if k <= levels:
+                bit = self.orders[part][k - 1]
+                length = self.lengths[k]
+                send_at = self.offsets[k - 1][part] + (1 - self.bit_of[bit]) * length
+                copies.append(self.copy(self.time_ref.at[rows_of(send_at, length)], self.recv_refs[sem], sem, bit))
+            else:
+                level = 2 * levels - k
+                bit = self.orders[part][level]
+                rows = self.weighted_ref.at[rows_of(self.offsets[level + 1][part], self.lengths[level + 1])]
+                copies.append(self.copy(rows, rows, sem, bit))
+        return copies
+
+    def start(self, k):
+        for copy in self.stage(k):
+            copy.start()
+
+    def finish(self, k):
+        levels = self.bits - 1
+        copies = self.stage(k)
+        for part in range(2):
+            if part < len(copies):
+                copies[part].wait()
+            if k <= levels:
+                length = self.lengths[k]
+                rows = rows_of(self.offsets[k][part], length)
+                if k == 0:
+                    self.time_ref[rows, :] += self.recv_refs[0][part * length : (part + 1) * length, :]
+                else:
+                    self.time_ref[rows, :] += self.recv_refs[2 * k - 1 + part][...]
+            if k == levels:
+                piece = min(length, self.steps)
+                for j in range(length // piece):
+                    at = self.offsets[k][part] + j * piece
+                    noise = self.noise_ref[rows_of(lax.rem(at, self.steps), piece), :]
+                    self.weighted_ref[rows_of(at, piece), :] = self.time_ref[rows_of(at, piece), :] * noise
+
+
 def normal_operator(
     bits,
     table_k_ref,
     inverse_t_ref,
     inverse_f_ref,
     hist_ref,
-    noise_ref,
+    noise_a_ref,
+    noise_b_ref,
     khat_ref,
     out_ref,
     hreal_ref,
     himag_ref,
-    spec_ref,
+    spec_a_ref,
+    spec_b_ref,
     grad_ref,
-    time_ref,
-    weighted_ref,
+    time_a_ref,
+    time_b_ref,
+    weighted_a_ref,
+    weighted_b_ref,
     partial_ref,
     from_left_ref,
     from_right_ref,
     *comm,
 ):
-    recv_refs, (send_sem, recv_sem, right_sems, left_sems) = comm[:-4], comm[-4:]
+    sems = comm[-6:]
+    right_sems, left_sems = sems[4:]
+    recv_count = (len(comm) - 6) // 2
     step = pl.program_id(0)
-    half_steps = pl.num_programs(0) // 2
+    phase = pl.num_programs(0) // 4
     blocks, vectors, part_params, steps = hist_ref.shape
     params = blocks * part_params
-    freq_block, _, sensors, _ = khat_ref.shape
-    total = vectors * steps
-    me = lax.axis_index("col")
-    bit_of = [lax.rem(me // 2**b, 2) for b in range(bits)]
-    partner = [me + (1 - 2 * bit_of[b]) * 2**b for b in range(bits)]
-    orders = col_steps(bits)
+    freq_block, _, _, half, _ = khat_ref.shape
+    pairs = vectors // 2
+    lanes = 2 * half
+    spec_refs = (spec_a_ref, spec_b_ref)
+    time_refs = (time_a_ref, time_b_ref)
+    weighted_refs = (weighted_a_ref, weighted_b_ref)
+    reduces = [
+        AllReduce(
+            bits, half, time_refs[h], weighted_refs[h], (noise_a_ref, noise_b_ref)[h],
+            comm[h * recv_count : (h + 1) * recv_count], sems[2 * h], sems[2 * h + 1],
+        )
+        for h in range(2)
+    ]
+    stages = 2 * bits
 
     @pl.when(step == 0)
     def _():
         barrier = pltpu.get_barrier_semaphore()
         for b in range(bits):
-            pl.semaphore_signal(barrier, inc=1, device_id={"col": partner[b]}, device_id_type=MESH)
+            pl.semaphore_signal(barrier, inc=1, device_id={"col": reduces[0].partner[b]}, device_id_type=MESH)
         greet_row(lax.axis_index("row"), blocks - 1, bits)
 
         for r in range(0, vectors, 2):
@@ -229,30 +330,29 @@
             spec = matmul_nt(table_k_ref[...], jnp.concatenate([high, low, high], axis=1))
             for j in range(2):
                 cols = slice(j * params, (j + 1) * params)
-                hreal_ref[pl.ds(r + j, steps, stride=vectors), :] = spec[:steps, cols]
-                himag_ref[pl.ds(r + j, steps, stride=vectors), :] = spec[steps:, cols]
-
-    @pl.when(step < half_steps)
-    def _():
+                rows = pl.ds(j * pairs + r // 2, steps, stride=vectors)
+                hreal_ref[rows, :] = spec[:steps, cols]
+                himag_ref[rows, :] = spec[steps:, cols]
+
+    def forward(h):
         for i in range(freq_block):
-            f = step * freq_block + i
+            f = lax.rem(step, phase) * freq_block + i
             rows = pl.ds(pl.multiple_of(f * vectors, vectors), vectors)
             real, imag = hreal_ref[rows, :], himag_ref[rows, :]
-            both = jnp.concatenate(
-                [jnp.concatenate([real, -imag], axis=1), jnp.concatenate([imag, real], axis=1)], axis=0
-            )
+            top, bottom = jnp.concatenate([real, -imag], axis=1), jnp.concatenate([imag, real], axis=1)
+            both = jnp.concatenate([top[:pairs], bottom[:pairs], top[pairs:], bottom[pairs:]], axis=0)
             lhs = jnp.concatenate(split(both), axis=0)
-            res = matmul_nt(lhs, khat_ref[i].reshape(2 * sensors, 2 * params))
-            top, bottom = res[: 2 * vectors], res[2 * vectors :]
-            spec_ref[pl.ds(pl.multiple_of(f * 2 * vectors, 2 * vectors), 2 * vectors), :] = (
-                top[:, :sensors] + (top[:, sensors:] + bottom[:, :sensors])
-            )
-
-    def to_time(r):
+            res = matmul_nt(lhs, khat_ref[i, 0].reshape(lanes, 2 * params))
+            high, low = res[: 2 * vectors], res[2 * vectors :]
+            data = high[:, :half] + (high[:, half:] + low[:, :half])
+            spec_refs[h][rows, :] = jnp.concatenate([data[:vectors], data[vectors:]], axis=1)
+
+    def to_time(h, pair):
+        spec_ref = spec_refs[h]
         spec = jnp.concatenate(
             [
                 jnp.concatenate(
-                    [spec_ref[pl.ds(part * vectors + r + j, steps, stride=2 * vectors), :] for j in range(2)],
+                    [spec_ref[pl.ds(part * pairs + pair + j, steps, stride=vectors), :] for j in range(2)],
                     axis=1,
                 )
                 for part in range(2)
@@ -262,120 +362,107 @@
         high, low = split(spec)
         times = matmul(inverse_t_ref[...], jnp.concatenate([high, low, high], axis=0))
         for j in range(2):
-            rows = pl.ds(pl.multiple_of((r + j) * steps, steps), steps)
-            time_ref[rows, :] = times[:, j * sensors : (j + 1) * sensors]
-
-    def to_spectrum(r):
-        rows = [pl.ds(pl.multiple_of((r + j) * steps, steps), steps) for j in range(2)]
-        high, low = split(jnp.concatenate([weighted_ref[rows[j], :] for j in range(2)], axis=1))
+            time_refs[h][rows_of((pair + j) * steps, steps), :] = times[:, j * lanes : (j + 1) * lanes]
+
+    def to_spectrum(h, pair):
+        weighted = [weighted_refs[h][rows_of((pair + j) * steps, steps), :] for j in range(2)]
+        high, low = split(jnp.concatenate(weighted, axis=1))
         spec = matmul(table_k_ref[...], jnp.concatenate([high, low, high], axis=0))
         for j in range(2):
-            cols = slice(j * sensors, (j + 1) * sensors)
-            spec_ref[pl.ds(r + j, steps, stride=2 * vectors), :] = spec[:steps, cols]
-            spec_ref[pl.ds(vectors + r + j, steps, stride=2 * vectors), :] = spec[steps:, cols]
-
-    @pl.when(step == half_steps - 1)
-    def _():
-        def rows_of(offset, length):
-            return pl.ds(pl.multiple_of(offset, 8), length)
-
-        def exchange(src, dst, sem, bit):
-            copy = pltpu.make_async_remote_copy(
-                src_ref=src,
-                dst_ref=dst,
-                send_sem=send_sem.at[sem],
-                recv_sem=recv_sem.at[sem],
-                device_id={"col": partner[bit]},
-                device_id_type=MESH,
-            )
-            copy.start()
-            return copy
-
-        half = vectors // 2
-        keep, give = bit_of[0] * half, (1 - bit_of[0]) * half
-
-        def give_body(j, carry):
-            to_time(give + 2 * j)
+            cols = slice(j * lanes, (j + 1) * lanes)
+            spec_refs[h][pl.ds(pair + j, steps, stride=vectors), :] = spec[:steps, cols]
+            spec_refs[h][pl.ds(pairs + pair + j, steps, stride=vectors), :] = spec[steps:, cols]
+
+    def over_pairs(body, h, first):
+        def one(j, carry):
+            body(h, first + 2 * j)
             return carry
 
-        def keep_body(j, carry):
-            to_time(keep + 2 * j)
-            return carry
-
-        lax.fori_loop(0, half // 2, give_body, 0)
-        length = total // 2
-        first = exchange(time_ref.at[rows_of(give * steps, length)], recv_refs[0], 0, 0)
-        lax.fori_loop(0, half // 2, keep_body, 0)
-        first.wait()
-
-        length //= 2
-        offsets = [keep * steps, keep * steps + length]
-        for part in range(2):
-            rows = rows_of(offsets[part], length)
-            time_ref[rows, :] += recv_refs[0][part * length : (part + 1) * length, :]
-        sem = 1
-        for level in range(bits - 1):
-            length //= 2
-            copies = []
-            for part in range(2):
-                bit = orders[part][level]
-                send_at = offsets[part] + (1 - bit_of[bit]) * length
-                offsets[part] = offsets[part] + bit_of[bit] * length
-                copies.append(exchange(time_ref.at[rows_of(send_at, length)], recv_refs[sem], sem, bit))
-                sem += 1
-            for part in range(2):
-                copies[part].wait()
-                rows = rows_of(offsets[part], length)
-                time_ref[rows, :] += recv_refs[sem - 2 + part][...]
-
-        piece = min(length, steps)
-        for part in range(2):
-            for j in range(length // piece):
-                at = offsets[part] + j * piece
-                noise = noise_ref[rows_of(lax.rem(at, steps), piece), :]
-                weighted_ref[rows_of(at, piece), :] = time_ref[rows_of(at, piece), :] * noise
-
-        for level in reversed(range(bits - 1)):
-            copies = []
-            for part in range(2):
-                bit = orders[part][level]
-                rows = weighted_ref.at[rows_of(offsets[part], length)]
-                copies.append(exchange(rows, rows, sem, bit))
-                sem += 1
-            for part in range(2):
-                copies[part].wait()
-                offsets[part] = offsets[part] - bit_of[orders[part][level]] * length
-            length *= 2
-        rows = weighted_ref.at[rows_of(keep * steps, 2 * length)]
-        last = exchange(rows, rows, sem, 0)
-
-        def keep_spectrum(j, carry):
-            to_spectrum(keep + 2 * j)
-            return carry
-
-        def give_spectrum(j, carry):
-            to_spectrum(give + 2 * j)
-            return carry
-
-        lax.fori_loop(0, half // 2, keep_spectrum, 0)
-        last.wait()
-        lax.fori_loop(0, half // 2, give_spectrum, 0)
-
-    @pl.when(step >= half_steps)
-    def _():
+        lax.fori_loop(0, pairs // 4, one, 0)
+
+    def begin(h):
+        reduce = reduces[h]
+        over_pairs(to_time, h, (1 - reduce.bit_of[0]) * (pairs // 2))
+        reduce.start(0)
+        over_pairs(to_time, h, reduce.bit_of[0] * (pairs // 2))
+
+    def end(h):
+        reduce = reduces[h]
+        over_pairs(to_spectrum, h, reduce.bit_of[0] * (pairs // 2))
+        reduce.finish(stages - 1)
+        over_pairs(to_spectrum, h, (1 - reduce.bit_of[0]) * (pairs // 2))
+
+    shares = [1.9] + [1 + 2.6 / 2**level for level in range(bits - 1)]
+    shares = shares + shares[::-1]
+
+    def events(h, base):
+        done = 0.0
+        for k in range(1, stages):
+            done += shares[k - 1]
+
+            @pl.when(step == base + jnp.minimum((int(1024 * done / sum(shares)) * phase + 1023) // 1024, phase - 1))
+            def _():
+                reduces[h].finish(k - 1)
+                reduces[h].start(k)
+
+    def backward(h):
         for i in range(freq_block):
-            f = (step - half_steps) * freq_block + i
+            f = lax.rem(step, phase) * freq_block + i
             base = pl.multiple_of(f * 2 * vectors, 2 * vectors)
-            high, low = split(spec_ref[pl.ds(base, 2 * vectors), :])
-            lhs = jnp.concatenate(
-                [jnp.concatenate([high, high], axis=1), jnp.concatenate([low, jnp.zeros_like(low)], axis=1)], axis=0
-            )
-            res = matmul(lhs, khat_ref[i].reshape(2 * sensors, 2 * params))
+            mine = spec_refs[h][pl.ds(pl.multiple_of(f * vectors, vectors), vectors), :]
+            swapped = jnp.concatenate([mine[:, half:], mine[:, :half]], axis=1)
+            left = lax.broadcasted_iota(jnp.int32, mine.shape, 1) < half
+            both = jnp.concatenate([jnp.where(left, mine, swapped), jnp.where(left, swapped, mine)], axis=0)
+            high, low = split(both)
+            left = lax.broadcasted_iota(jnp.int32, both.shape, 1) < half
+            low = jnp.where(left, low.astype(f32), 0.0).astype(bf16)
+            res = matmul(jnp.concatenate([high, low], axis=0), khat_ref[i, 0].reshape(lanes, 2 * params))
             res = res[: 2 * vectors] + res[2 * vectors :]
-            grad_ref[pl.ds(base, vectors), :] = res[:vectors, :params] + res[vectors:, params:]
-            grad_ref[pl.ds(base + vectors, vectors), :] = res[vectors:, :params] - res[:vectors, params:]
-
-    @pl.when(step == 2 * half_steps - 1)
+            real = jnp.concatenate([res[:pairs], res[vectors : vectors + pairs]], axis=0)
+            imag = jnp.concatenate([res[pairs:vectors], res[vectors + pairs :]], axis=0)
+            grad_real = real[:, :params] + imag[:, params:]
+            grad_imag = imag[:, :params] - real[:, params:]
+            if h == 0:
+                grad_ref[pl.ds(base, vectors), :] = grad_real
+                grad_ref[pl.ds(base + vectors, vectors), :] = grad_imag
+            else:
+                grad_ref[pl.ds(base, vectors), :] += grad_real
+                grad_ref[pl.ds(base + vectors, vectors), :] += grad_imag
+
+    @pl.when(step < phase)
+    def _():
+        forward(0)
+
+    @pl.when(step == phase - 1)
+    def _():
+        begin(0)
+
+    events(0, phase)
+
+    @pl.when((step >= phase) & (step < 2 * phase))
+    def _():
+        forward(1)
+
+    @pl.when(step == 2 * phase - 1)
+    def _():
+        begin(1)
+        end(0)
+
+    events(1, 2 * phase)
+
+    @pl.when((step >= 2 * phase) & (step < 3 * phase))
+    def _():
+        backward(0)
+
+    @pl.when(step == 3 * phase - 1)
+    def _():
+        end(1)
+
+    @pl.when(step >= 3 * phase)
+    def _():
+        backward(1)
+
+    @pl.when(step == 4 * phase - 1)
     def _():
         chunk = vectors // CHUNKS
         last = blocks - 1
@@ -385,7 +472,10 @@
             spec = jnp.concatenate(
                 [
                     jnp.concatenate(
-                        [grad_ref[pl.ds(part * vectors + r + j, steps, stride=2 * vectors), :] for part in range(2)],
+                        [
+                            grad_ref[pl.ds(part * vectors + j * pairs + r // 2, steps, stride=2 * vectors), :]
+                            for part in range(2)
+                        ],
                         axis=0,
                     ).T
                     for j in range(2)
@@ -477,6 +567,7 @@
 
     moved = history.transpose(1, 0, 2)
     hops = CHUNKS * (row_count - 1)
+    per_half = sensors // 2 // SENSOR_BLOCK
     anywhere = pl.BlockSpec(memory_space=pl.ANY)
     khat, gathered = pl.pallas_call(
         functools.partial(kernel_transform, row_count),
@@ -487,11 +578,13 @@
             anywhere,
         ],
         out_specs=[
-            pl.BlockSpec((steps, 2, SENSOR_BLOCK, 2 * params), lambda i: (0, 0, i, 0)),
+            pl.BlockSpec(
+                (steps, 1, 2, SENSOR_BLOCK, 2 * params), lambda i: (0, i // per_half, 0, lax.rem(i, per_half), 0)
+            ),
             anywhere,
         ],
         out_shape=[
-            jax.ShapeDtypeStruct((steps, 2, sensors, 2 * params), bf16),
+            jax.ShapeDtypeStruct((steps, 2, 2, sensors // 2, 2 * params), bf16),
             jax.ShapeDtypeStruct((row_count, vectors, part_params, steps), f32),
         ],
         scratch_shapes=[
@@ -514,36 +607,42 @@
 
     bits = col_count.bit_length() - 1
     total = vectors * steps
-    lengths = [total // 2]
+    rows = total // 2
+    lengths = [rows // 2]
     for level in range(bits - 1):
-        lengths += [total >> (level + 3)] * 2
-    half_steps = steps // FREQ_BLOCK
+        lengths += [rows >> (level + 3)] * 2
+    phase = steps // FREQ_BLOCK
+    noise = noise_weight.T
+    noise_halves = [jnp.tile(noise[:, h * sensors // 2 : (h + 1) * sensors // 2], (1, 2)) for h in range(2)]
     gradient = pl.pallas_call(
         functools.partial(normal_operator, bits),
-        grid=(2 * half_steps,),
+        grid=(4 * phase,),
         in_specs=[
             whole(2 * steps, 3 * steps),
             whole(steps, 6 * steps),
             whole(6 * steps, steps),
             whole(row_count, vectors, part_params, steps),
             whole(steps, sensors),
-            pl.BlockSpec((FREQ_BLOCK, 2, sensors, 2 * params), lambda i: (lax.rem(i, half_steps), 0, 0, 0)),
+            whole(steps, sensors),
+            pl.BlockSpec(
+                (FREQ_BLOCK, 1, 2, sensors // 2, 2 * params),
+                lambda i: (lax.rem(i, phase), lax.rem(i // phase, 2), 0, 0, 0),
+            ),
         ],
         out_specs=whole(vectors, part_params, steps),
         out_shape=jax.ShapeDtypeStruct((vectors, part_params, steps), f32),
         scratch_shapes=[
             pltpu.VMEM((steps * vectors, params), f32),
             pltpu.VMEM((steps * vectors, params), f32),
-            pltpu.VMEM((steps * 2 * vectors, sensors), f32),
+            pltpu.VMEM((steps * vectors, sensors), f32),
+            pltpu.VMEM((steps * vectors, sensors), f32),
             pltpu.VMEM((steps * 2 * vectors, params), f32),
-            pltpu.VMEM((total, sensors), f32),
-            pltpu.VMEM((total, sensors), f32),
+            *[pltpu.VMEM((rows, sensors), f32)] * 4,
             pltpu.VMEM((row_count, vectors, part_params, steps), f32),
             pltpu.VMEM((row_count - 1, vectors, part_params, steps), f32),
             pltpu.VMEM((row_count - 1, vectors, part_params, steps), f32),
-            *[pltpu.VMEM((length, sensors), f32) for length in lengths],
-            pltpu.SemaphoreType.DMA((2 * len(lengths),)),
-            pltpu.SemaphoreType.DMA((2 * len(lengths),)),
+            *[pltpu.VMEM((length, sensors), f32) for length in lengths] * 2,
+            *[pltpu.SemaphoreType.DMA((2 * len(lengths),))] * 4,
             pltpu.SemaphoreType.DMA((2, hops)),
             pltpu.SemaphoreType.DMA((2, hops)),
         ],
@@ -556,7 +655,7 @@
             transcendentals=0,
         ),
         name="normal_operator",
-    )(table_k, inverse_t, inverse_f, gathered, noise_weight.T, khat)
+    )(table_k, inverse_t, inverse_f, gathered, *noise_halves, khat)
 
     return gradient.transpose(1, 0, 2) + prior_weight[:, None, None] * history
 

time: 162 us -> 160 us (0.988)
  Pallas kernels: 155 us -> 153 us
    unnamed x16 -> x7, local copies, waits for them, and re-layouts: 4.84 us -> 2.15 us
    pallas_call x1, Pallas kernels: 113 us -> 110 us  [local(): pl.pallas_call(functools.partial(normal_operator, bits), grid=(4 * phase,...]
where the time goes in v4:
time: 160 us
  Pallas kernels  153 us (96%)
  local copies, waits for them, and re-layouts  4.81 us (3%)
    pallas_call x1, Pallas kernels, local(): pl.pallas_call(functools.partial(normal_operator, bits), grid=(4 * phase,...  110 us
    pallas_call x1, Pallas kernels, local(): pl.pallas_call(functools.partial(kernel_transform, row_count), grid=(sens...  43 us

profile of v4, /device:TPU:0, one launch (start us, length us, event | category | flops | bytes accessed | tf_op | source)
XLA Modules:
  0.0 159.6 jit_solution(7668876275635573980)
XLA Ops:
  0.0 2.1 %copy.20 = f32[32,16,256]{2,0,1:T(8,128)} copy(f32[32,16,256]{2,1,0:T(8,128)} %param.8) | data formatting | bytes 1048576 | tf_op args[1]
  2.1 0.0 copy-start.1
  2.1 43.0 %kernel_transform.1 = (bf16[256,2,2,64,256]{4,3,2,1,0:T(8,128)(2,1)}, f32[4,16,32,256]{3,2,1,0:T(8,128)}) custom-call(bf16[512,768]{1,0:T(8,128)(2,1)} %constant.6.clone.table_ref.table_k_ref, f32[128,128,256]{2,1,0:T(8,128)} %kernel_ref.1, f32[16,32,256]{2,1,0:T(8,128)} %bitcast.8), custom_call_target="tpu_custom_call" | custom-call | flops 12884901888 | bytes 50331648 | tf_op jit(solution)/shard_map/kernel_transform/pallas_call | solution.py:572
  45.2 0.0 copy-done.1
  45.2 0.8 copy.14.noise_a_ref
  46.0 0.8 copy.15.noise_b_ref
  46.8 0.0 copy-start
  46.8 0.0 copy-start.2
  46.8 110.3 %normal_operator.1 = f32[16,32,256]{2,1,0:T(8,128)} custom-call(bf16[512,768]{1,0:T(8,128)(2,1)} %constant.6.clone.table_ref.table_k_ref, bf16[256,1536]{1,0:T(8,128)(2,1)} %constant.7.clone.inverse_t_ref, bf16[1536,256]{1,0:T(8,128)(2,1)} %constant.8.clone.inverse_f_ref, f32[4,16,32,256]{3,2,1,0:T(8,128)} %get-tuple-element.7.hist_ref, ...), custom_call_target="tpu_custom_call" | custom-call | flops 2147483648 | bytes 67108864 | tf_op jit(solution)/shard_map/normal_operator/pallas_call | solution.py:617
  157.1 0.0 copy-done
  157.1 0.0 copy-done.2
  157.1 1.4 bitcast_add_fusion
  158.5 1.1 copy.17
  (3 shorter events, 0.0 us)
Async XLA Ops:
  2.1 43.1 %copy-start.1 = (f32[128,256]{1,0:T(8,128)S(1)}, f32[128,256]{1,0:T(8,128)}, u32[]{:S(2)}) copy-start(f32[128,256]{1,0:T(8,128)} %param.9) | copy-start | bytes 393220
  46.8 110.3 %copy-start = (f32[32,16,256]{2,1,0:T(8,128)S(1)}, f32[32,16,256]{2,1,0:T(8,128)}, u32[]{:S(2)}) copy-start(f32[32,16,256]{2,1,0:T(8,128)} %param.8) | copy-start | bytes 1572868
  46.8 110.3 %copy-start.2 = (f32[32]{0:T(128)S(1)}, f32[32]{0:T(128)}, u32[]{:S(2)}) copy-start(f32[32]{0:T(128)} %param.10) | copy-start | bytes 388

commit v5 on v4

--- a/solution.py
+++ b/solution.py
@@ -15,6 +15,7 @@
 VMEM_LIMIT = 60 * 1024 * 1024
 SENSOR_BLOCK = 16
 FREQ_BLOCK = 32
+GROUP = 8
 
 
 def transform_table(steps):
@@ -71,8 +72,9 @@
 
 
 def kernel_transform(
-    row_count, table_ref, kernel_ref, hist_ref, out_ref, all_ref, real_ref, imag_ref, own_sem, right_sems, left_sems
+    row_count, table_ref, kernel_ref, raw_ref, out_ref, all_ref, hist_ref, real_ref, imag_ref, *sems
 ):
+    own_sem, right_sems, left_sems = sems
     sensors, params, steps = kernel_ref.shape
     grid_step = pl.program_id(0)
     grid_steps = pl.num_programs(0)
@@ -130,6 +132,7 @@
 
     @pl.when(grid_step == 0)
     def _():
+        hist_ref[...] = jnp.swapaxes(raw_ref[...], 0, 1)
         greet_row(me, last)
         for c in range(CHUNKS):
             start_hop(0, c)
@@ -189,9 +192,9 @@
 
 
 class AllReduce:
-    def __init__(self, bits, half_sensors, time_ref, weighted_ref, noise_ref, recv_refs, send_sem, recv_sem):
+    def __init__(self, bits, sensors, time_ref, weighted_ref, noise_ref, recv_refs, send_sem, recv_sem):
         me = lax.axis_index("col")
-        self.bits, self.steps = bits, noise_ref.shape[0]
+        self.bits, self.steps, self.sensors = bits, noise_ref.shape[0], sensors
         self.time_ref, self.weighted_ref, self.noise_ref = time_ref, weighted_ref, noise_ref
         self.recv_refs, self.send_sem, self.recv_sem = recv_refs, send_sem, recv_sem
         self.bit_of = [lax.rem(me // 2**b, 2) for b in range(bits)]
@@ -267,7 +270,8 @@
                 piece = min(length, self.steps)
                 for j in range(length // piece):
                     at = self.offsets[k][part] + j * piece
-                    noise = self.noise_ref[rows_of(lax.rem(at, self.steps), piece), :]
+                    noise = self.noise_ref[rows_of(lax.rem(at, self.steps), piece), :][:, self.sensors]
+                    noise = jnp.concatenate([noise, noise], axis=1)
                     self.weighted_ref[rows_of(at, piece), :] = self.time_ref[rows_of(at, piece), :] * noise
 
 
@@ -277,12 +281,12 @@
     inverse_t_ref,
     inverse_f_ref,
     hist_ref,
-    noise_a_ref,
-    noise_b_ref,
+    weights_ref,
     khat_ref,
     out_ref,
     hreal_ref,
     himag_ref,
+    noise_ref,
     spec_a_ref,
     spec_b_ref,
     grad_ref,
@@ -310,7 +314,7 @@
     weighted_refs = (weighted_a_ref, weighted_b_ref)
     reduces = [
         AllReduce(
-            bits, half, time_refs[h], weighted_refs[h], (noise_a_ref, noise_b_ref)[h],
+            bits, slice(h * half, (h + 1) * half), time_refs[h], weighted_refs[h], noise_ref,
             comm[h * recv_count : (h + 1) * recv_count], sems[2 * h], sems[2 * h + 1],
         )
         for h in range(2)
@@ -324,6 +328,7 @@
             pl.semaphore_signal(barrier, inc=1, device_id={"col": reduces[0].partner[b]}, device_id_type=MESH)
         greet_row(lax.axis_index("row"), blocks - 1, bits)
 
+        noise_ref[...] = weights_ref[...].T
         for r in range(0, vectors, 2):
             hist = jnp.concatenate([hist_ref[:, r + j].reshape(params, steps) for j in range(2)], axis=0)
             high, low = split(hist)
@@ -334,8 +339,14 @@
                 hreal_ref[rows, :] = spec[:steps, cols]
                 himag_ref[rows, :] = spec[steps:, cols]
 
+    def grouped(product):
+        for first in range(0, freq_block, GROUP):
+            stores = [product(first + i) for i in range(GROUP)]
+            for ref, rows, value in sum(stores, []):
+                ref[rows, :] = value
+
     def forward(h):
-        for i in range(freq_block):
+        def product(i):
             f = lax.rem(step, phase) * freq_block + i
             rows = pl.ds(pl.multiple_of(f * vectors, vectors), vectors)
             real, imag = hreal_ref[rows, :], himag_ref[rows, :]
@@ -345,7 +356,9 @@
             res = matmul_nt(lhs, khat_ref[i, 0].reshape(lanes, 2 * params))
             high, low = res[: 2 * vectors], res[2 * vectors :]
             data = high[:, :half] + (high[:, half:] + low[:, :half])
-            spec_refs[h][rows, :] = jnp.concatenate([data[:vectors], data[vectors:]], axis=1)
+            return [(spec_refs[h], rows, jnp.concatenate([data[:vectors], data[vectors:]], axis=1))]
+
+        grouped(product)
 
     def to_time(h, pair):
         spec_ref = spec_refs[h]
@@ -406,7 +419,7 @@
                 reduces[h].start(k)
 
     def backward(h):
-        for i in range(freq_block):
+        def product(i):
             f = lax.rem(step, phase) * freq_block + i
             base = pl.multiple_of(f * 2 * vectors, 2 * vectors)
             mine = spec_refs[h][pl.ds(pl.multiple_of(f * vectors, vectors), vectors), :]
@@ -420,14 +433,13 @@
             res = res[: 2 * vectors] + res[2 * vectors :]
             real = jnp.concatenate([res[:pairs], res[vectors : vectors + pairs]], axis=0)
             imag = jnp.concatenate([res[pairs:vectors], res[vectors + pairs :]], axis=0)
-            grad_real = real[:, :params] + imag[:, params:]
-            grad_imag = imag[:, :params] - real[:, params:]
-            if h == 0:
-                grad_ref[pl.ds(base, vectors), :] = grad_real
-                grad_ref[pl.ds(base + vectors, vectors), :] = grad_imag
-            else:
-                grad_ref[pl.ds(base, vectors), :] += grad_real
-                grad_ref[pl.ds(base + vectors, vectors), :] += grad_imag
+            values = [real[:, :params] + imag[:, params:], imag[:, :params] - real[:, params:]]
+            rows = [pl.ds(base, vectors), pl.ds(base + vectors, vectors)]
+            if h == 1:
+                values = [value + grad_ref[at, :] for value, at in zip(values, rows)]
+            return [(grad_ref, at, value) for value, at in zip(values, rows)]
+
+        grouped(product)
 
     @pl.when(step < phase)
     def _():
@@ -536,7 +548,7 @@
             return carry
 
         lax.fori_loop(1, blocks, line_body, 0)
-        out_ref[...] = partial_ref[row]
+        out_ref[...] = jnp.swapaxes(partial_ref[row], 0, 1)
 
         for right in (True, False):
             behind = row if right else last - row
@@ -565,7 +577,6 @@
 
     whole = lambda *shape: pl.BlockSpec(shape, lambda i: (0,) * len(shape))
 
-    moved = history.transpose(1, 0, 2)
     hops = CHUNKS * (row_count - 1)
     per_half = sensors // 2 // SENSOR_BLOCK
     anywhere = pl.BlockSpec(memory_space=pl.ANY)
@@ -575,7 +586,7 @@
         in_specs=[
             whole(2 * steps, 3 * steps),
             pl.BlockSpec((SENSOR_BLOCK, params, steps), lambda i: (i, 0, 0)),
-            anywhere,
+            whole(part_params, vectors, steps),
         ],
         out_specs=[
             pl.BlockSpec(
@@ -588,6 +599,7 @@
             jax.ShapeDtypeStruct((row_count, vectors, part_params, steps), f32),
         ],
         scratch_shapes=[
+            pltpu.VMEM((vectors, part_params, steps), f32),
             pltpu.VMEM((steps * SENSOR_BLOCK, params), f32),
             pltpu.VMEM((steps * SENSOR_BLOCK, params), f32),
             pltpu.SemaphoreType.DMA,
@@ -603,7 +615,7 @@
             transcendentals=0,
         ),
         name="kernel_transform",
-    )(table_k, kernel, moved)
+    )(table_k, kernel, history)
 
     bits = col_count.bit_length() - 1
     total = vectors * steps
@@ -612,8 +624,6 @@
     for level in range(bits - 1):
         lengths += [rows >> (level + 3)] * 2
     phase = steps // FREQ_BLOCK
-    noise = noise_weight.T
-    noise_halves = [jnp.tile(noise[:, h * sensors // 2 : (h + 1) * sensors // 2], (1, 2)) for h in range(2)]
     gradient = pl.pallas_call(
         functools.partial(normal_operator, bits),
         grid=(4 * phase,),
@@ -622,18 +632,18 @@
             whole(steps, 6 * steps),
             whole(6 * steps, steps),
             whole(row_count, vectors, part_params, steps),
-            whole(steps, sensors),
-            whole(steps, sensors),
+            whole(sensors, steps),
             pl.BlockSpec(
                 (FREQ_BLOCK, 1, 2, sensors // 2, 2 * params),
                 lambda i: (lax.rem(i, phase), lax.rem(i // phase, 2), 0, 0, 0),
             ),
         ],
-        out_specs=whole(vectors, part_params, steps),
-        out_shape=jax.ShapeDtypeStruct((vectors, part_params, steps), f32),
+        out_specs=whole(part_params, vectors, steps),
+        out_shape=jax.ShapeDtypeStruct((part_params, vectors, steps), f32),
         scratch_shapes=[
             pltpu.VMEM((steps * vectors, params), f32),
             pltpu.VMEM((steps * vectors, params), f32),
+            pltpu.VMEM((steps, sensors), f32),
             pltpu.VMEM((steps * vectors, sensors), f32),
             pltpu.VMEM((steps * vectors, sensors), f32),
             pltpu.VMEM((steps * 2 * vectors, params), f32),
@@ -655,9 +665,9 @@
             transcendentals=0,
         ),
         name="normal_operator",
-    )(table_k, inverse_t, inverse_f, gathered, *noise_halves, khat)
-
-    return gradient.transpose(1, 0, 2) + prior_weight[:, None, None] * history
+    )(table_k, inverse_t, inverse_f, gathered, noise_weight, khat)
+
+    return gradient + prior_weight[:, None, None] * history
 
 
 def solution(mesh):

time: 160 us -> 156 us (0.975)
  local copies, waits for them, and re-layouts: 4.81 us -> 0.01 us
    unnamed x7 -> x4, local copies, waits for them, and re-layouts: 2.15 us -> 0.01 us
where the time goes in v5:
time: 156 us; the launch traced here: 155 us
  Pallas kernels  153 us (98%)
  other arithmetic  1.95 us (1%)
    pallas_call x1, Pallas kernels, local(): pl.pallas_call(functools.partial(normal_operator, bits), grid=(4 * phase,...  110 us
    pallas_call x1, Pallas kernels, local(): pl.pallas_call(functools.partial(kernel_transform, row_count), grid=(sens...  43.1 us

profile of v5, /device:TPU:0, one launch (start us, length us, event | category | flops | bytes accessed | tf_op | source)
XLA Modules:
  0.0 155.4 jit_solution(14023636504106843547)
XLA Ops:
  0.0 43.1 %kernel_transform.1 = (bf16[256,2,2,64,256]{4,3,2,1,0:T(8,128)(2,1)}, f32[4,16,32,256]{3,2,1,0:T(8,128)}) custom-call(bf16[512,768]{1,0:T(8,128)(2,1)} %constant.6.clone.table_ref.table_k_ref, f32[128,128,256]{2,1,0:T(8,128)} %kernel_ref.1, f32[32,16,256]{2,1,0:T(8,128)} %raw_ref.1), custom_call_target="tpu_custom_call" | custom-call | flops 12884901888 | bytes 50331648 | tf_op jit(solution)/shard_map/kernel_transform/pallas_call | solution.py:583
  43.1 0.0 copy-start
  43.1 0.0 copy-start.1
  43.2 110.3 %normal_operator.1 = f32[32,16,256]{2,1,0:T(8,128)} custom-call(bf16[512,768]{1,0:T(8,128)(2,1)} %constant.6.clone.table_ref.table_k_ref, bf16[256,1536]{1,0:T(8,128)(2,1)} %constant.7.clone.inverse_t_ref, bf16[1536,256]{1,0:T(8,128)(2,1)} %constant.8.clone.inverse_f_ref, f32[4,16,32,256]{3,2,1,0:T(8,128)} %get-tuple-element.7.hist_ref, ...), custom_call_target="tpu_custom_call" | custom-call | flops 2147483648 | bytes 67108864 | tf_op jit(solution)/shard_map/normal_operator/pallas_call | solution.py:627
  153.5 0.0 copy-done
  153.5 0.0 copy-done.1
  153.5 2.0 %multiply_add_fusion = f32[32,16,256]{2,1,0:T(8,128)} fusion(f32[32,16,256]{2,1,0:T(8,128)} %normal_operator.1, f32[32,16,256]{2,1,0:T(8,128)S(1)} %copy-done, f32[32]{0:T(128)S(1)} %copy-done.1), kind=kLoop, calls=%fused_computation | loop fusion | flops 262144 | bytes 1572992 | tf_op jit(solution)/shard_map/add | solution.py:670
Async XLA Ops:
  43.1 110.3 %copy-start = (f32[32,16,256]{2,1,0:T(8,128)S(1)}, f32[32,16,256]{2,1,0:T(8,128)}, u32[]{:S(2)}) copy-start(f32[32,16,256]{2,1,0:T(8,128)} %raw_ref.1) | copy-start | bytes 1572868
  43.1 110.3 %copy-start.1 = (f32[32]{0:T(128)S(1)}, f32[32]{0:T(128)}, u32[]{:S(2)}) copy-start(f32[32]{0:T(128)} %param.10) | copy-start | bytes 388

commit v6 on v5

--- a/solution.py
+++ b/solution.py
@@ -152,18 +152,19 @@
         spec = matmul_nt(table_ref[...], jnp.concatenate([high, low, high], axis=1))
         for j in range(2):
             cols = slice(j * params, (j + 1) * params)
-            real_ref[pl.ds(s + j, steps, stride=sensors), :] = spec[:steps, cols]
-            imag_ref[pl.ds(s + j, steps, stride=sensors), :] = spec[steps:, cols]
+            real_ref[pl.ds(s + j, steps, stride=sensors + 1), :] = spec[:steps, cols]
+            imag_ref[pl.ds(s + j, steps, stride=sensors + 1), :] = spec[steps:, cols]
 
     group = 8
 
     def emit(i, carry):
-        rows = pl.ds(pl.multiple_of(i * group * sensors, group * sensors), group * sensors)
-        freqs = pl.ds(i * group, group)
+        base = pl.multiple_of(i * group * (sensors + 1), group)
         for part, ref in enumerate((real_ref, imag_ref)):
-            high, low = split(ref[rows, :].reshape(group, sensors, params))
-            out_ref[freqs, 0, 0, :, part * params : (part + 1) * params] = high
-            out_ref[freqs, 0, 1, :, part * params : (part + 1) * params] = low
+            cols = slice(part * params, (part + 1) * params)
+            for g in range(group):
+                high, low = split(ref[pl.ds(base + g * (sensors + 1), sensors), :])
+                out_ref[i * group + g, 0, 0, :, cols] = high
+                out_ref[i * group + g, 0, 1, :, cols] = low
         return carry
 
     lax.fori_loop(0, steps // group, emit, 0)
@@ -335,7 +336,7 @@
             spec = matmul_nt(table_k_ref[...], jnp.concatenate([high, low, high], axis=1))
             for j in range(2):
                 cols = slice(j * params, (j + 1) * params)
-                rows = pl.ds(j * pairs + r // 2, steps, stride=vectors)
+                rows = pl.ds(j * pairs + r // 2, steps, stride=vectors + 1)
                 hreal_ref[rows, :] = spec[:steps, cols]
                 himag_ref[rows, :] = spec[steps:, cols]
 
@@ -348,7 +349,7 @@
     def forward(h):
         def product(i):
             f = lax.rem(step, phase) * freq_block + i
-            rows = pl.ds(pl.multiple_of(f * vectors, vectors), vectors)
+            rows = pl.ds(f * (vectors + 1), vectors)
             real, imag = hreal_ref[rows, :], himag_ref[rows, :]
             top, bottom = jnp.concatenate([real, -imag], axis=1), jnp.concatenate([imag, real], axis=1)
             both = jnp.concatenate([top[:pairs], bottom[:pairs], top[pairs:], bottom[pairs:]], axis=0)
@@ -365,7 +366,7 @@
         spec = jnp.concatenate(
             [
                 jnp.concatenate(
-                    [spec_ref[pl.ds(part * pairs + pair + j, steps, stride=vectors), :] for j in range(2)],
+                    [spec_ref[pl.ds(part * pairs + pair + j, steps, stride=vectors + 1), :] for j in range(2)],
                     axis=1,
                 )
                 for part in range(2)
@@ -383,8 +384,8 @@
         spec = matmul(table_k_ref[...], jnp.concatenate([high, low, high], axis=0))
         for j in range(2):
             cols = slice(j * lanes, (j + 1) * lanes)
-            spec_refs[h][pl.ds(pair + j, steps, stride=vectors), :] = spec[:steps, cols]
-            spec_refs[h][pl.ds(pairs + pair + j, steps, stride=vectors), :] = spec[steps:, cols]
+            spec_refs[h][pl.ds(pair + j, steps, stride=vectors + 1), :] = spec[:steps, cols]
+            spec_refs[h][pl.ds(pairs + pair + j, steps, stride=vectors + 1), :] = spec[steps:, cols]
 
     def over_pairs(body, h, first):
         def one(j, carry):
@@ -421,8 +422,8 @@
     def backward(h):
         def product(i):
             f = lax.rem(step, phase) * freq_block + i
-            base = pl.multiple_of(f * 2 * vectors, 2 * vectors)
-            mine = spec_refs[h][pl.ds(pl.multiple_of(f * vectors, vectors), vectors), :]
+            base = f * (2 * vectors + 1)
+            mine = spec_refs[h][pl.ds(f * (vectors + 1), vectors), :]
             swapped = jnp.concatenate([mine[:, half:], mine[:, :half]], axis=1)
             left = lax.broadcasted_iota(jnp.int32, mine.shape, 1) < half
             both = jnp.concatenate([jnp.where(left, mine, swapped), jnp.where(left, swapped, mine)], axis=0)
@@ -485,7 +486,7 @@
                 [
                     jnp.concatenate(
                         [
-                            grad_ref[pl.ds(part * vectors + j * pairs + r // 2, steps, stride=2 * vectors), :]
+                            grad_ref[pl.ds(part * vectors + j * pairs + r // 2, steps, stride=2 * vectors + 1), :]
                             for part in range(2)
                         ],
                         axis=0,
@@ -600,8 +601,8 @@
         ],
         scratch_shapes=[
             pltpu.VMEM((vectors, part_params, steps), f32),
-            pltpu.VMEM((steps * SENSOR_BLOCK, params), f32),
-            pltpu.VMEM((steps * SENSOR_BLOCK, params), f32),
+            pltpu.VMEM(((steps + 1) * (SENSOR_BLOCK + 1), params), f32),
+            pltpu.VMEM(((steps + 1) * (SENSOR_BLOCK + 1), params), f32),
             pltpu.SemaphoreType.DMA,
             pltpu.SemaphoreType.DMA((2, hops)),
             pltpu.SemaphoreType.DMA((2, hops)),
@@ -641,12 +642,12 @@
         out_specs=whole(part_params, vectors, steps),
         out_shape=jax.ShapeDtypeStruct((part_params, vectors, steps), f32),
         scratch_shapes=[
-            pltpu.VMEM((steps * vectors, params), f32),
-            pltpu.VMEM((steps * vectors, params), f32),
+            pltpu.VMEM(((steps + 1) * (vectors + 1), params), f32),
+            pltpu.VMEM(((steps + 1) * (vectors + 1), params), f32),
             pltpu.VMEM((steps, sensors), f32),
-            pltpu.VMEM((steps * vectors, sensors), f32),
-            pltpu.VMEM((steps * vectors, sensors), f32),
-            pltpu.VMEM((steps * 2 * vectors, params), f32),
+            pltpu.VMEM(((steps + 1) * (vectors + 1), sensors), f32),
+            pltpu.VMEM(((steps + 1) * (vectors + 1), sensors), f32),
+            pltpu.VMEM(((steps + 1) * (2 * vectors + 1), params), f32),
             *[pltpu.VMEM((rows, sensors), f32)] * 4,
             pltpu.VMEM((row_count, vectors, part_params, steps), f32),
             pltpu.VMEM((row_count - 1, vectors, part_params, steps), f32),

time: 156 us -> 153 us (0.981)
  Pallas kernels: 153 us -> 150 us
    pallas_call x1, Pallas kernels: 110 us -> 107 us  [local(): pl.pallas_call(functools.partial(normal_operator, bits), grid=(4 * phase,...]
where the time goes in v6:
time: 153 us; the launch traced here: 152 us
  Pallas kernels  150 us (98%)
  other arithmetic  1.95 us (1%)
    pallas_call x1, Pallas kernels, local(): pl.pallas_call(functools.partial(normal_operator, bits), grid=(4 * phase,...  107 us
    pallas_call x1, Pallas kernels, local(): pl.pallas_call(functools.partial(kernel_transform, row_count), grid=(sens...  43.1 us

profile of v6, /device:TPU:0, one launch (start us, length us, event | category | flops | bytes accessed | tf_op | source)
XLA Modules:
  0.0 152.1 jit_solution(15298605079348243358)
XLA Ops:
  0.0 43.1 %kernel_transform.1 = (bf16[256,2,2,64,256]{4,3,2,1,0:T(8,128)(2,1)}, f32[4,16,32,256]{3,2,1,0:T(8,128)}) custom-call(bf16[512,768]{1,0:T(8,128)(2,1)} %constant.6.clone.table_ref.table_k_ref, f32[128,128,256]{2,1,0:T(8,128)} %kernel_ref.1, f32[32,16,256]{2,1,0:T(8,128)} %raw_ref.1), custom_call_target="tpu_custom_call" | custom-call | flops 12884901888 | bytes 50331648 | tf_op jit(solution)/shard_map/kernel_transform/pallas_call | solution.py:584
  43.1 0.0 copy-start
  43.1 0.0 copy-start.1
  43.2 107.0 %normal_operator.1 = f32[32,16,256]{2,1,0:T(8,128)} custom-call(bf16[512,768]{1,0:T(8,128)(2,1)} %constant.6.clone.table_ref.table_k_ref, bf16[256,1536]{1,0:T(8,128)(2,1)} %constant.7.clone.inverse_t_ref, bf16[1536,256]{1,0:T(8,128)(2,1)} %constant.8.clone.inverse_f_ref, f32[4,16,32,256]{3,2,1,0:T(8,128)} %get-tuple-element.7.hist_ref, ...), custom_call_target="tpu_custom_call" | custom-call | flops 2147483648 | bytes 67108864 | tf_op jit(solution)/shard_map/normal_operator/pallas_call | solution.py:628
  150.2 0.0 copy-done
  150.2 0.0 copy-done.1
  150.2 2.0 %multiply_add_fusion = f32[32,16,256]{2,1,0:T(8,128)} fusion(f32[32,16,256]{2,1,0:T(8,128)} %normal_operator.1, f32[32,16,256]{2,1,0:T(8,128)S(1)} %copy-done, f32[32]{0:T(128)S(1)} %copy-done.1), kind=kLoop, calls=%fused_computation | loop fusion | flops 262144 | bytes 1572992 | tf_op jit(solution)/shard_map/add | solution.py:671
Async XLA Ops:
  43.1 107.0 %copy-start = (f32[32,16,256]{2,1,0:T(8,128)S(1)}, f32[32,16,256]{2,1,0:T(8,128)}, u32[]{:S(2)}) copy-start(f32[32,16,256]{2,1,0:T(8,128)} %raw_ref.1) | copy-start | bytes 1572868
  43.1 107.0 %copy-start.1 = (f32[32]{0:T(128)S(1)}, f32[32]{0:T(128)}, u32[]{:S(2)}) copy-start(f32[32]{0:T(128)} %param.10) | copy-start | bytes 388
